TPU v7x, 32 devices: a whole 2x2x4 slice. The times are simulated.
32 devices in a mesh: rows: 8 (over z, y), bank: 4 (over x, core).
Axes of the slice: x: 2, y: 2, z: 4, core: 2. Of those that a mesh axis runs over, the one named last changes fastest.
Arguments:
- hidden_in: bfloat16 [32768, 512], P(('rows', 'bank')), may hold values from -6 to 6
- lengths: int32 [32, 16], P(('rows', 'bank')), may hold values from 0 to 1024, as said below
- ln1_gain: float32 [512], replicated, may hold values from 0.1 to 1.9
- ln1_bias: float32 [512], replicated, may hold values from -3 to 3
- w_qkv: bfloat16 [512, 1536], replicated, may hold values from -0.25 to 0.25
- w_out: bfloat16 [512, 512], replicated, may hold values from -0.75 to 0.75
- b_out: float32 [512], replicated, may hold values from -3 to 3
- ln2_gain: float32 [512], replicated, may hold values from 0.1 to 1.9
- ln2_bias: float32 [512], replicated, may hold values from -3 to 3
- w_up: bfloat16 [512, 2048], replicated, may hold values from -0.25 to 0.25
- b_up: float32 [2048], replicated, may hold values from -3 to 3
- w_down: bfloat16 [2048, 512], replicated, may hold values from -0.125 to 0.125
- b_down: float32 [512], replicated, may hold values from -3 to 3
- bank: bfloat16 [8192, 512], P('bank'), may hold values from -6 to 6
- bank_labels: int32 [8192], P('bank'), may hold values from 0 to 203
- target_slots: int32 [32768], P(('rows', 'bank')), may hold values from 0 to 8191
- gold_ids: int32 [32768], P(('rows', 'bank')), may hold values from 0 to 203
Outputs:
- block_out: bfloat16 [32768, 512], P(('rows', 'bank'))
- token_loss: float32 [32768], P(('rows', 'bank'))
- input_grad: bfloat16 [32768, 512], P(('rows', 'bank'))
- ln1_gain_grad: float32 [512], replicated
- ln1_bias_grad: float32 [512], replicated
- w_qkv_grad: float32 [512, 1536], replicated
- w_out_grad: float32 [512, 512], replicated
- b_out_grad: float32 [512], replicated
- ln2_gain_grad: float32 [512], replicated
- ln2_bias_grad: float32 [512], replicated
- w_up_grad: float32 [512, 2048], replicated
- b_up_grad: float32 [2048], replicated
- w_down_grad: float32 [2048, 512], replicated
- b_down_grad: float32 [512], replicated
Inputs may be any that keep to these rules, and one draw needn't show every extreme that they name: Each row's lengths sum to at most 1024; zeros may follow the last document; in some row one document fills all 1024 slots.
All inputs are finite; a program needn't handle non-finite values.
Results may differ from a plain program's by a relative error of at most 0.01225.
Values may be sent and summed in bfloat16 or wider, within the bound.
No kernel may reach another device: no remote copies, remote signals or barrier semaphores. Data moves between devices by JAX's collectives and lax.ppermute only.
A program may use at most 256 MiB of HBM per device.

v0:
```python
import math

import jax
import jax.numpy as jnp
from jax import lax
from jax.sharding import PartitionSpec as P

HEADS = 8
HEAD_DIM = 64


def layout(lengths_row, length):
    doc_ends = jnp.cumsum(lengths_row)
    places = jnp.arange(length, dtype=jnp.int32)
    passed = (places[:, None] >= doc_ends[None, :]).astype(jnp.int32)
    segment = jnp.sum(passed, axis=1)
    begins = jnp.sum(passed * lengths_row[None, :], axis=1)
    return (segment, places - begins, places < doc_ends[-1])


def sinusoid(offset, width):
    half_idx = jnp.arange(width // 2, dtype=jnp.float32)
    inv_freq = jnp.exp(half_idx * (-2.0 * math.log(10000.0) / width))
    angles = offset.astype(jnp.float32)[:, None] * inv_freq[None, :]
    return jnp.concatenate([jnp.sin(angles), jnp.cos(angles)], axis=1)


def norm_forward(values, gain_row, shift_row):
    center = values - jnp.mean(values, axis=1, keepdims=True)
    inv_std = lax.rsqrt(jnp.mean(center * center, axis=1, keepdims=True) + 1e-05)
    unit_rows = center * inv_std
    return (unit_rows * gain_row + shift_row, unit_rows, inv_std)


def norm_backward(grad_norm, gain_row, unit_rows, inv_std):
    grad_unit = grad_norm * gain_row
    grad_input = inv_std * (
        grad_unit
        - jnp.mean(grad_unit, axis=1, keepdims=True)
        - unit_rows * jnp.mean(grad_unit * unit_rows, axis=1, keepdims=True)
    )
    return (grad_input, jnp.sum(grad_norm * unit_rows, axis=0), jnp.sum(grad_norm, axis=0))


def head_scores(head_query, head_key, allowed):
    raw_scores = jnp.einsum(
        "qd,kd->qk", head_query, head_key, preferred_element_type=jnp.float32
    ) / math.sqrt(HEAD_DIM)
    return jnp.where(allowed, raw_scores, -1e30)


def slot_stats(query_rows, bank_rows, label_rows, slot_ids, gold_rows, target_rows):
    scores = jnp.einsum(
        "qd,sd->qs", query_rows, bank_rows, preferred_element_type=jnp.float32
    ) / math.sqrt(query_rows.shape[1])
    positive = (label_rows[None, :] == gold_rows[:, None]) | (
        slot_ids[None, :] == target_rows[:, None]
    )
    top_all = jnp.max(scores, axis=1)
    sum_all = jnp.sum(jnp.exp(scores - top_all[:, None]), axis=1)
    masked = jnp.where(positive, scores, -1e30)
    top_pos = jnp.max(masked, axis=1)
    sum_pos = jnp.sum(jnp.where(positive, jnp.exp(masked - top_pos[:, None]), 0.0), axis=1)
    return (scores, positive, (top_all, sum_all, top_pos, sum_pos))


def score_grads(scores, positive, live_rows, lse_all, lse_pos):
    dist_all = jnp.exp(scores - lse_all[:, None])
    dist_pos = jnp.where(positive, jnp.exp(scores - lse_pos[:, None]), 0.0)
    return (live_rows[:, None] * (dist_all - dist_pos)).astype(jnp.bfloat16)


def body(
    hidden_in,
    lengths,
    ln1_gain,
    ln1_bias,
    w_qkv,
    w_out,
    b_out,
    ln2_gain,
    ln2_bias,
    w_up,
    b_up,
    w_down,
    b_down,
    bank,
    bank_labels,
    target_slots,
    gold_ids,
):
    length = hidden_in.shape[0]
    width = hidden_in.shape[1]
    segment, offset, live_flag = layout(lengths[0], length)
    live_rows = live_flag.astype(jnp.float32)
    stream = hidden_in.astype(jnp.float32) + sinusoid(offset, width)
    normed_a, unit_a, inv_a = norm_forward(stream, ln1_gain, ln1_bias)
    normed_a = normed_a.astype(jnp.bfloat16)
    projected = jnp.dot(normed_a, w_qkv, preferred_element_type=jnp.float32).astype(jnp.bfloat16)
    places = jnp.arange(length, dtype=jnp.int32)
    allowed = (places[:, None] >= places[None, :]) & (segment[:, None] == segment[None, :])
    head_outputs = []
    head_lse = []
    for head_idx in range(HEADS):
        low_col = head_idx * HEAD_DIM
        head_query = projected[:, low_col : low_col + HEAD_DIM]
        head_key = projected[:, width + low_col : width + low_col + HEAD_DIM]
        head_value = projected[:, 2 * width + low_col : 2 * width + low_col + HEAD_DIM]
        scores = head_scores(head_query, head_key, allowed)
        row_top = jnp.max(scores, axis=1, keepdims=True)
        raised = jnp.exp(scores - row_top)
        row_sum = jnp.sum(raised, axis=1, keepdims=True)
        attn_probs = (raised / row_sum).astype(jnp.bfloat16)
        head_outputs.append(jnp.dot(attn_probs, head_value, preferred_element_type=jnp.float32))
        head_lse.append(row_top + jnp.log(row_sum))
    attn_mixed = jnp.concatenate(head_outputs, axis=1).astype(jnp.bfloat16)
    after_attn = stream + jnp.dot(attn_mixed, w_out, preferred_element_type=jnp.float32) + b_out
    normed_c, unit_c, inv_c = norm_forward(after_attn, ln2_gain, ln2_bias)
    normed_c = normed_c.astype(jnp.bfloat16)
    hidden = jnp.dot(normed_c, w_up, preferred_element_type=jnp.float32) + b_up
    activated = jax.nn.gelu(hidden, approximate=False).astype(jnp.bfloat16)
    result = after_attn + jnp.dot(activated, w_down, preferred_element_type=jnp.float32) + b_down
    queries_b = result.astype(jnp.bfloat16)
    bank_all, labels_all = (
        lax.all_gather(bank, "bank", axis=0, tiled=True),
        lax.all_gather(bank_labels, "bank", axis=0, tiled=True),
    )
    slot_ids = jnp.arange(bank_all.shape[0], dtype=jnp.int32)
    scores_b, positive, local_stats = slot_stats(
        queries_b, bank_all, labels_all, slot_ids, gold_ids, target_slots
    )
    lse_all = local_stats[0] + jnp.log(local_stats[1])
    lse_pos = local_stats[2] + jnp.log(local_stats[3])
    grad_scores = score_grads(scores_b, positive, live_rows, lse_all, lse_pos)
    grad_result = jnp.dot(grad_scores, bank_all, preferred_element_type=jnp.float32) / math.sqrt(
        width
    )
    token_loss = (lse_all - lse_pos) * live_rows
    grad_b_down = jnp.sum(grad_result, axis=0)
    grad_out_low = grad_result.astype(jnp.bfloat16)
    grad_w_down = jnp.einsum(
        "tf,td->fd", activated, grad_out_low, preferred_element_type=jnp.float32
    )
    grad_act = jnp.einsum("td,fd->tf", grad_out_low, w_down, preferred_element_type=jnp.float32)
    gelu_pull = jax.vjp(lambda pre_act: jax.nn.gelu(pre_act, approximate=False), hidden)[1]
    grad_hidden = gelu_pull(grad_act)[0]
    grad_b_up = jnp.sum(grad_hidden, axis=0)
    grad_hidden_low = grad_hidden.astype(jnp.bfloat16)
    grad_w_up = jnp.einsum(
        "td,tf->df", normed_c, grad_hidden_low, preferred_element_type=jnp.float32
    )
    grad_normed_c = jnp.einsum(
        "tf,df->td", grad_hidden_low, w_up, preferred_element_type=jnp.float32
    )
    grad_mid, grad_ln2_gain, grad_ln2_bias = norm_backward(grad_normed_c, ln2_gain, unit_c, inv_c)
    grad_after = grad_result + grad_mid
    grad_b_out = jnp.sum(grad_after, axis=0)
    grad_after_low = grad_after.astype(jnp.bfloat16)
    grad_w_out = jnp.einsum(
        "td,te->de", attn_mixed, grad_after_low, preferred_element_type=jnp.float32
    )
    grad_mixed = jnp.einsum(
        "te,de->td", grad_after_low, w_out, preferred_element_type=jnp.float32
    ).astype(jnp.bfloat16)
    grad_query_parts = []
    grad_key_parts = []
    grad_value_parts = []
    for head_idx in range(HEADS):
        low_col = head_idx * HEAD_DIM
        head_query = projected[:, low_col : low_col + HEAD_DIM]
        head_key = projected[:, width + low_col : width + low_col + HEAD_DIM]
        head_value = projected[:, 2 * width + low_col : 2 * width + low_col + HEAD_DIM]
        head_grad = grad_mixed[:, low_col : low_col + HEAD_DIM]
        scores = head_scores(head_query, head_key, allowed)
        soft_rows = jnp.exp(scores - head_lse[head_idx])
        grad_probs = jnp.einsum(
            "qd,kd->qk", head_grad, head_value, preferred_element_type=jnp.float32
        )
        grad_head_scores = (
            soft_rows * (grad_probs - jnp.sum(grad_probs * soft_rows, axis=1, keepdims=True))
        ).astype(jnp.bfloat16)
        grad_query_parts.append(
            jnp.dot(grad_head_scores, head_key, preferred_element_type=jnp.float32)
            / math.sqrt(HEAD_DIM)
        )
        grad_key_parts.append(
            jnp.einsum(
                "qk,qd->kd", grad_head_scores, head_query, preferred_element_type=jnp.float32
            )
            / math.sqrt(HEAD_DIM)
        )
        grad_value_parts.append(
            jnp.einsum(
                "qk,qd->kd",
                soft_rows.astype(jnp.bfloat16),
                head_grad,
                preferred_element_type=jnp.float32,
            )
        )
    grad_projected = jnp.concatenate(
        grad_query_parts + grad_key_parts + grad_value_parts, axis=1
    ).astype(jnp.bfloat16)
    grad_w_qkv = jnp.einsum(
        "td,te->de", normed_a, grad_projected, preferred_element_type=jnp.float32
    )
    grad_normed_a = jnp.einsum(
        "te,de->td", grad_projected, w_qkv, preferred_element_type=jnp.float32
    )
    grad_front, grad_ln1_gain, grad_ln1_bias = norm_backward(grad_normed_a, ln1_gain, unit_a, inv_a)
    input_grad = (grad_after + grad_front).astype(jnp.bfloat16)
    (
        grad_w_qkv,
        grad_w_out,
        grad_b_out,
        grad_ln1_gain,
        grad_ln1_bias,
        grad_w_up,
        grad_b_up,
        grad_w_down,
        grad_b_down,
        grad_ln2_gain,
        grad_ln2_bias,
    ) = lax.psum(
        (
            grad_w_qkv,
            grad_w_out,
            grad_b_out,
            grad_ln1_gain,
            grad_ln1_bias,
            grad_w_up,
            grad_b_up,
            grad_w_down,
            grad_b_down,
            grad_ln2_gain,
            grad_ln2_bias,
        ),
        ("rows", "bank"),
    )
    return (
        queries_b,
        token_loss,
        input_grad,
        grad_ln1_gain,
        grad_ln1_bias,
        grad_w_qkv,
        grad_w_out,
        grad_b_out,
        grad_ln2_gain,
        grad_ln2_bias,
        grad_w_up,
        grad_b_up,
        grad_w_down,
        grad_b_down,
    )


def solution(mesh):
    in_specs = (
        P(("rows", "bank"), None),
        P(("rows", "bank"), None),
        P(),
        P(),
        P(),
        P(),
        P(),
        P(),
        P(),
        P(),
        P(),
        P(),
        P(),
        P("bank", None),
        P("bank"),
        P(("rows", "bank")),
        P(("rows", "bank")),
    )
    out_specs = (
        P(("rows", "bank"), None),
        P(("rows", "bank")),
        P(("rows", "bank"), None),
        P(),
        P(),
        P(),
        P(),
        P(),
        P(),
        P(),
        P(),
        P(),
        P(),
        P(),
    )
    return jax.shard_map(body, mesh=mesh, in_specs=in_specs, out_specs=out_specs, check_vma=False)
```

profile of v0, /device:TPU:0, one launch (start us, length us, event | category | flops | bytes accessed | tf_op | source)
XLA Modules:
  0.0 573.3 jit_solution(4903604782119601411)
XLA Ops:
  11.7 3.7 multiply_sine_fusion
  28.0 6.2 %all_gather.7 = s32[8192]{0:T(1024)S(1)} all-gather(s32[2048]{0:T(1024)S(1)} %copy-done.62), channel_id=1, replica_groups=mesh['rows'=8,'bank'=4] {'bank'}, dimensions={0}, use_global_device_ids=true | all-gather | bytes 40960 | tf_op jit(solution)/shard_map/all_gather | solution.py:126
  53.6 23.6 %multiply_convert_fusion.2 = (bf16[1024,2048]{1,0:T(8,128)(2,1)S(1)}, f32[1024,2048]{1,0:T(8,128)}, f32[1024,2048]{1,0:T(8,128)}) fusion(f32[2048]{0:T(1024)S(1)} %copy-done.71, bf16[512,2048]{1,0:T(8,128)(2,1)S(1)} %copy-done, f32[1024,512]{0,1:T(8,128)S(1)} %get-tuple-element.122, f32[512]{0:T(512)S(1)} %copy-done.73, f32[512]{0:T(512)S(1)} %copy-done.61, ...), kind=kOutput, calls=%fused_computation.12 | convolution fusion | flops 2288517120 | bytes 25186304 | tf_op jit(solution)/shard_map/dot_general | solution.py:120
  81.7 26.7 %fusion.1 = (f32[1024]{0:T(1024)S(1)}, f32[1024]{0:T(1024)S(1)}, f32[1024,8192]{1,0:T(8,128)}) fusion(s32[1024]{0:T(1024)S(1)} %copy-done.65, s32[8192]{0:T(1024)S(1)} %all_gather.7, s32[1024]{0:T(1024)S(1)} %copy-done.66, bf16[1024,512]{0,1:T(8,128)(2,1)S(1)} %add_convert_fusion.1, bf16[8192,512]{1,0:T(8,128)(2,1)} %all-gather.2.cloned.1.call-done), kind=kOutput, calls=%fused_computation.7 | convolution fusion | flops 8648652800 | bytes 43040768 | tf_op jit(solution)/shard_map/qd,sd->qs/dot_general | solution.py:53
  108.4 20.9 %select_reduce_fusion = (f32[1024]{0:T(1024)S(1)}, f32[1024]{0:T(1024)S(1)}) fusion(f32[1024,8192]{1,0:T(8,128)} %get-tuple-element.124, f32[1024]{0:T(1024)S(1)} %get-tuple-element.72, s32[1024]{0:T(1024)S(1)} %copy-done.65, s32[8192]{0:T(1024)S(1)} %all_gather.7, s32[1024]{0:T(1024)S(1)} %copy-done.66, f32[1024]{0:T(1024)S(1)} %get-tuple-element.73), kind=kLoop, calls=%fused_computation.1 | loop fusion | flops 83884032 | bytes 33611776 | tf_op jit(solution)/shard_map/reduce_sum | solution.py:63
  130.6 29.6 %fusion.2 = f32[1024,512]{0,1:T(8,128)} fusion(bf16[8192,512]{1,0:T(8,128)(2,1)} %all-gather.2.cloned.1.call-done, f32[1024,8192]{1,0:T(8,128)} %get-tuple-element.124, f32[1024]{0:T(1024)S(1)} %get-tuple-element.96, f32[1024]{0:T(1024)S(1)} %get-tuple-element.97, f32[1024]{0:T(1024)S(1)} %fusion.234, s32[1024]{0:T(1024)S(1)} %copy-done.65, ...), kind=kOutput, calls=%fused_computation.8 | convolution fusion | flops 8673820672 | bytes 44093440 | tf_op jit(solution)/shard_map/dot_general | solution.py:135
  160.2 7.3 %fusion.161 = f32[2048,512]{1,0:T(8,128)} fusion(bf16[1024,2048]{1,0:T(8,128)(2,1)} %copy-done.76, f32[1024,512]{0,1:T(8,128)} %fusion.2), kind=kOutput, calls=%fused_computation.226 | convolution fusion | flops 2148532224 | bytes 10485760 | tf_op jit(solution)/shard_map/tf,td->fd/dot_general | solution.py:141
  167.6 8.8 %fusion.255 = (f32[2048]{0:T(1024)S(1)}, bf16[1024,2048]{1,0:T(8,128)(2,1)S(1)}) fusion(f32[1024,2048]{1,0:T(8,128)} %get-tuple-element.99, bf16[2048,512]{1,0:T(8,128)(2,1)S(1)} %copy-done.69, f32[1024,512]{0,1:T(8,128)S(1)} %copy-done.45, f32[1024,2048]{1,0:T(8,128)} %get-tuple-element.123, f32[2048]{0:T(1024)S(1)} %copy-done.71), kind=kOutput, calls=%fused_computation.344 | convolution fusion | flops 2182084608 | bytes 25182208 | tf_op jit(solution)/shard_map/td,fd->tf/dot_general | solution.py:144
  176.4 3.7 fusion.254
  180.1 4.5 fusion.50
  224.8 5.9 %multiply_convert_fusion.10 = bf16[1024,1024]{0,1:T(8,128)(2,1)} fusion(f32[1024,1024]{0,1:T(8,128)} %get-tuple-element.126, f32[1024,1024]{0,1:T(8,128)} %copy-done.15, f32[1024]{0:T(1024)S(1)} %get-tuple-element.125, f32[1024]{0:T(1024)S(1)} %copy-done.56), kind=kLoop, calls=%fused_computation.47 | loop fusion | flops 4194304 | bytes 10493952 | tf_op jit(solution)/shard_map/convert_element_type | solution.py:181
  233.5 4.8 multiply_convert_fusion.3
  238.3 4.7 multiply_convert_fusion.4
  243.0 4.6 multiply_convert_fusion.5
  247.6 4.7 multiply_convert_fusion.6
  252.3 4.6 multiply_convert_fusion.7
  256.9 4.7 multiply_convert_fusion.8
  261.6 4.6 multiply_convert_fusion.9
  315.1 5.5 fusion.239
  323.2 5.6 fusion.253
  328.7 3.2 copy.66
  339.2 42.8 %all-reduce = (f32[512]{0:T(512)}, f32[512]{0:T(512)}, f32[512]{0:T(512)}, f32[512]{0:T(512)}, f32[512]{0:T(512)}, /*index=5*/f32[2048]{0:T(1024)}, f32[512]{0:T(512)}) all-reduce(f32[512]{0:T(512)S(1)} %get-tuple-element.76, f32[512]{0:T(512)S(1)} %get-tuple-element.141, ...), channel_id=1, replica_groups=mesh['rows'=8,'bank'=4] {'rows','bank'}, use_global_device_ids=true, to_apply=%region_40.41 | all-reduce | flops 5120 | bytes 40960 | tf_op jit(solution)/shard_map/psum | solution.py:223
  382.0 173.7 %all-reduce.4.cloned.1.call-done = (f32[512,1536]{1,0:T(8,128)}, f32[512,512]{1,0:T(8,128)}, f32[512,2048]{1,0:T(8,128)}, f32[2048,512]{1,0:T(8,128)}) async-done(((f32[512,1536]{1,0:T(8,128)}, f32[512,512]{1,0:T(8,128)}, f32[512,2048]{1,0:T(8,128)}, f32[2048,512]{1,0:T(8,128)}), (f32[512,1536]{1,0:T(8,128)}, f32[512,512]{1,0:T(8,128)}, f32[512,2048]{1,0:T(8,128)}, ...) | async-done | bytes 12582928 | tf_op jit(solution)/shard_map/psum | solution.py:223
  555.7 3.9 copy.107
  (258 shorter events, 150.0 us)
Async XLA Ops:
  7.2 46.4 %copy-start = (bf16[512,2048]{1,0:T(8,128)(2,1)S(1)}, bf16[512,2048]{1,0:T(8,128)(2,1)}, u32[]{:S(2)}) copy-start(bf16[512,2048]{1,0:T(8,128)(2,1)} %param.26) | copy-start | bytes 6291460
  7.2 74.4 %all-gather.2.cloned.1.call-start = ((), (), s32[]{:S(2)}) async-start(), calls=%async_computation | async-start | bytes 10485760 | tf_op jit(solution)/shard_map/all_gather | solution.py:125
  7.9 547.7 %all-reduce.4.cloned.1.call-start = ((), (), s32[]{:S(2)}) async-start(), calls=%async_computation.1 | async-start | bytes 25165824 | tf_op jit(solution)/shard_map/psum | solution.py:223
  15.8 31.2 %copy-start.18 = (f32[1024,512]{0,1:T(8,128)}, f32[1024,512]{0,1:T(8,128)S(1)}, u32[]{:S(2)}) copy-start(f32[1024,512]{0,1:T(8,128)S(1)} %get-tuple-element.101) | copy-start | bytes 6291460
  18.9 27.2 %copy-start.35 = (bf16[1024,1536]{1,0:T(8,128)(2,1)}, bf16[1024,1536]{1,0:T(8,128)(2,1)S(1)}, u32[]{:S(2)}) copy-start(bf16[1024,1536]{1,0:T(8,128)(2,1)S(1)} %convolution_convert_fusion) | copy-start | bytes 9437188
  20.0 26.1 %copy-start.1 = (f32[1024,1024]{0,1:T(8,128)}, f32[1024,1024]{0,1:T(8,128)S(1)}, u32[]{:S(2)}) copy-start(f32[1024,1024]{0,1:T(8,128)S(1)} %get-tuple-element.120) | copy-start | bytes 12582916
  21.0 24.2 %copy-start.3 = (f32[1024,1024]{0,1:T(8,128)}, f32[1024,1024]{0,1:T(8,128)S(1)}, u32[]{:S(2)}) copy-start(f32[1024,1024]{0,1:T(8,128)S(1)} %get-tuple-element.118) | copy-start | bytes 12582916
  22.1 22.2 %copy-start.5 = (f32[1024,1024]{0,1:T(8,128)}, f32[1024,1024]{0,1:T(8,128)S(1)}, u32[]{:S(2)}) copy-start(f32[1024,1024]{0,1:T(8,128)S(1)} %get-tuple-element.116) | copy-start | bytes 12582916
  23.2 20.3 %copy-start.7 = (f32[1024,1024]{0,1:T(8,128)}, f32[1024,1024]{0,1:T(8,128)S(1)}, u32[]{:S(2)}) copy-start(f32[1024,1024]{0,1:T(8,128)S(1)} %get-tuple-element.114) | copy-start | bytes 12582916
  24.3 18.2 %copy-start.9 = (f32[1024,1024]{0,1:T(8,128)}, f32[1024,1024]{0,1:T(8,128)S(1)}, u32[]{:S(2)}) copy-start(f32[1024,1024]{0,1:T(8,128)S(1)} %get-tuple-element.112) | copy-start | bytes 12582916
  25.8 14.5 %copy-start.11 = (f32[1024,1024]{0,1:T(8,128)}, f32[1024,1024]{0,1:T(8,128)S(1)}, u32[]{:S(2)}) copy-start(f32[1024,1024]{0,1:T(8,128)S(1)} %get-tuple-element.110) | copy-start | bytes 12582916
  26.9 12.5 %copy-start.13 = (f32[1024,1024]{0,1:T(8,128)}, f32[1024,1024]{0,1:T(8,128)S(1)}, u32[]{:S(2)}) copy-start(f32[1024,1024]{0,1:T(8,128)S(1)} %get-tuple-element.108) | copy-start | bytes 12582916
  28.0 7.7 %copy-start.15 = (f32[1024,1024]{0,1:T(8,128)}, f32[1024,1024]{0,1:T(8,128)S(1)}, u32[]{:S(2)}) copy-start(f32[1024,1024]{0,1:T(8,128)S(1)} %get-tuple-element.106) | copy-start | bytes 12582916
  48.2 29.0 %copy-start.23 = (f32[1024,512]{0,1:T(8,128)}, f32[1024,512]{0,1:T(8,128)S(1)}, u32[]{:S(2)}) copy-start(f32[1024,512]{0,1:T(8,128)S(1)} %get-tuple-element.122) | copy-start | bytes 6291460
  53.5 25.6 %copy-start.68 = (bf16[2048,512]{1,0:T(8,128)(2,1)S(1)}, bf16[2048,512]{1,0:T(8,128)(2,1)}, u32[]{:S(2)}) copy-start(bf16[2048,512]{1,0:T(8,128)(2,1)} %param.28) | copy-start | bytes 6291460
  53.6 25.6 %copy-start.72 = (f32[512]{0:T(512)S(1)}, f32[512]{0:T(512)}, u32[]{:S(2)}) copy-start(f32[512]{0:T(512)} %param.29) | copy-start | bytes 6148
  81.6 26.8 %copy-start.46 = (bf16[1024,512]{0,1:T(8,128)(2,1)}, bf16[1024,512]{0,1:T(8,128)(2,1)S(1)}, u32[]{:S(2)}) copy-start(bf16[1024,512]{0,1:T(8,128)(2,1)S(1)} %add_convert_fusion.1) | copy-start | bytes 3145732
  160.2 7.3 %copy-start.45 = (f32[1024,512]{0,1:T(8,128)S(1)}, f32[1024,512]{0,1:T(8,128)}, u32[]{:S(2)}) copy-start(f32[1024,512]{0,1:T(8,128)} %fusion.2) | copy-start | bytes 6291460
  160.2 7.3 %copy-start.69 = (bf16[2048,512]{1,0:T(8,128)(2,1)S(1)}, bf16[2048,512]{1,0:T(8,128)(2,1)}, u32[]{:S(2)}) copy-start(bf16[2048,512]{1,0:T(8,128)(2,1)} %param.28) | copy-start | bytes 6291460
  194.1 7.3 %copy-start.21 = (f32[1024,512]{0,1:T(8,128)}, f32[1024,512]{0,1:T(8,128)S(1)}, u32[]{:S(2)}) copy-start(f32[1024,512]{0,1:T(8,128)S(1)} %get-tuple-element.94) | copy-start | bytes 6291460
  198.4 23.4 %copy-start.37 = (bf16[1024,512]{0,1:T(8,128)(2,1)}, bf16[1024,512]{0,1:T(8,128)(2,1)S(1)}, u32[]{:S(2)}) copy-start(bf16[1024,512]{0,1:T(8,128)(2,1)S(1)} %convolution_convert_fusion.1) | copy-start | bytes 3145732
  281.4 7.2 %copy-start.32 = (bf16[1024,1024]{0,1:T(8,128)(2,1)S(1)}, bf16[1024,1024]{0,1:T(8,128)(2,1)}, u32[]{:S(2)}) copy-start(bf16[1024,1024]{0,1:T(8,128)(2,1)} %multiply_convert_fusion.8) | copy-start | bytes 6291460
  296.2 7.4 %copy-start.17 = (f32[1024,1024]{0,1:T(8,128)S(1)}, f32[1024,1024]{0,1:T(8,128)}, u32[]{:S(2)}) copy-start(f32[1024,1024]{0,1:T(8,128)} %copy-done.15) | copy-start | bytes 12582916
  296.2 7.4 %copy-start.38 = (bf16[1024,512]{0,1:T(8,128)(2,1)S(1)}, bf16[1024,512]{0,1:T(8,128)(2,1)}, u32[]{:S(2)}) copy-start(bf16[1024,512]{0,1:T(8,128)(2,1)} %copy-done.37) | copy-start | bytes 3145732
  (55 other events, 185.7 us)
Sparse Core Ops, SparseCore 0:
  9.6 61.1 all-gather.1
  320.8 234.8 all-reduce.3
where the time goes:
time: 583 us; the launch traced here: 573 us
  matrix products  214 us (37%)
  waiting for transfers between devices  174 us (30%)
  other arithmetic  88.6 us (15%)
  blocking collectives  49 us (8%)
  local copies, waits for them, and re-layouts  32.8 us (6%)
  between operations  14.9 us (3%)
    psum x1, waiting for transfers between devices, body(): lax.psum((grad_w_qkv, grad_w_out, grad_b_out, grad_ln1_gain, grad_ln1_bia...  174 us
    psum x1, blocking collectives, body(): lax.psum((grad_w_qkv, grad_w_out, grad_b_out, grad_ln1_gain, grad_ln1_bia...  42.8 us
    convert_element_type x8, other arithmetic, body(): grad_head_scores = (soft_rows * (grad_probs - jnp.sum(grad_probs * soft_r...  38.6 us
    dot_general x1, matrix products, body(): jnp.dot(grad_scores, bank_all, preferred_element_type=jnp.float32)  29.6 us
    dot_general x1, matrix products, slot_stats(): jnp.einsum('qd,sd->qs', query_rows, bank_rows, preferred_element_type=jnp...  26.7 us
    unnamed x161, local copies, waits for them, and re-layouts  25.3 us
    dot_general x1, matrix products, body(): hidden = jnp.dot(normed_c, w_up, preferred_element_type=jnp.float32) + b_up  23.6 us
    dot_general x8, matrix products, body(): jnp.einsum('qd,kd->qk', head_grad, head_value, preferred_element_type=jnp...  22.6 us
  transfers between devices with their start and end apart: 2, of which 1 were waited for; matrix products, arithmetic and copies ran while one was open for 14% of the time, Pallas kernels for 0%

commit v1 on v0

v1 whole, which is shorter than its diff:
```python
import functools
import math

import jax
import jax.numpy as jnp
import numpy as np
from jax import lax
from jax.experimental import pallas as pl
from jax.experimental.pallas import tpu as pltpu
from jax.sharding import PartitionSpec as P

LOG2E = 1.4426950408889634
LN2 = 0.6931471805599453
NT = (((1,), (1,)), ((), ()))
NN = (((1,), (0,)), ((), ()))
f32, bf16 = jnp.float32, jnp.bfloat16

def column(row, rows):
    return jnp.transpose(jnp.broadcast_to(row.astype(f32), (128, rows)))[:, :1]

def bank_kernel(lengths_ref, q_ref, gold_ref, target_ref, labels_ref, bank_hbm,
                grad_ref, loss_ref, bsum_ref,
                bank_ref, s0_ref, s1_ref, e_ref, max_ref, sems, *, rows, tile, docs):
    step = pl.program_id(0)
    slots, width = bank_ref.shape
    tiles = slots // tile
    c = LOG2E / math.sqrt(width)
    copies = [pltpu.make_async_copy(bank_hbm.at[pl.ds(j * tile, tile)], bank_ref.at[pl.ds(j * tile, tile)], sems.at[j]) for j in range(tiles)]

    @pl.when(step == 0)
    def _():
        for j in range(tiles):
            copies[j].start()

    total = lengths_ref[0, 0]
    for j in range(1, docs):
        total = total + lengths_ref[0, j]
    gold = column(gold_ref[...], rows)
    target = column(target_ref[...], rows)
    gold_b = jnp.broadcast_to(gold, (rows, 128)).astype(jnp.int32)
    target_b = jnp.broadcast_to(target, (rows, 128)).astype(jnp.int32)
    place = step * rows + lax.broadcasted_iota(jnp.int32, (rows, 1), 0)
    live = place < total
    q = q_ref[...]
    lane = lax.broadcasted_iota(jnp.int32, (1, tile), 1)

    def wide(col):
        return jnp.concatenate([col] * (tile // 128), axis=1)

    def positive_of(j):
        labels = labels_ref[j]
        return (labels == wide(gold_b)) | ((lane + j * tile) == wide(target_b))

    def scores(j):
        return lax.dot_general(q, bank_ref[pl.ds(j * tile, tile), :], NT, preferred_element_type=f32)

    def fold(x):
        out = x[:, :128]
        for i in range(1, tile // 128):
            out = out + x[:, i * 128:(i + 1) * 128]
        return out

    def fold_max(x):
        out = x[:, :128]
        for i in range(1, tile // 128):
            out = jnp.maximum(out, x[:, i * 128:(i + 1) * 128])
        return out

    def eat(j, s_ref, top, sum_all, sum_pos):
        s = s_ref[...]
        here = jnp.max(fold_max(s), axis=1, keepdims=True) * c
        new_top = jnp.maximum(top, here)
        shrink = jnp.exp2(top - new_top)
        e = jnp.exp2(s * c - new_top)
        pos = positive_of(j)
        sum_all = sum_all * shrink + fold(e)
        sum_pos = sum_pos * shrink + fold(jnp.where(pos, e, 0.0))
        e_ref[j] = e.astype(e_ref.dtype)
        max_ref[j] = new_top
        return new_top, sum_all, sum_pos

    @pl.when(step == 0)
    def _():
        copies[0].wait()
    s0_ref[...] = scores(0)
    state = (jnp.full((rows, 1), -1e30, f32), jnp.zeros((rows, 128), f32), jnp.zeros((rows, 128), f32))

    bufs = (s0_ref, s1_ref)
    for j in range(tiles):
        if j + 1 < tiles:
            @pl.when(step == 0)
            def _():
                copies[j + 1].wait()
            bufs[(j + 1) % 2][...] = scores(j + 1)
        state = eat(j, bufs[j % 2], *state)
    top, sum_all, sum_pos = state
    sum_all = jnp.sum(sum_all, axis=1, keepdims=True)
    sum_pos = jnp.sum(sum_pos, axis=1, keepdims=True)
    safe = jnp.min(sum_pos) >= 2.0 ** -60
    lse_all = top + jnp.log2(sum_all)

    def finish(loss, acc):
        loss_ref[...] = jnp.transpose(jnp.broadcast_to(jnp.where(live, loss, 0.0), (rows, 128)))[:1, :]
        acc = acc * (1.0 / math.sqrt(width))
        grad_ref[...] = acc
        part = jnp.sum(acc, axis=0, keepdims=True)
        bsum_ref[...] = jnp.where(step == 0, part, bsum_ref[...] + part)

    @pl.when(safe)
    def _():
        lse_pos = top + jnp.log2(sum_pos)
        inv_all = jnp.where(live, 1.0 / sum_all, 0.0)
        inv_diff = inv_all - jnp.where(live, 1.0 / sum_pos, 0.0)
        acc = jnp.zeros((rows, width), f32)
        for j in range(tiles):
            factor = jnp.exp2(max_ref[j] - top)
            on = jnp.broadcast_to(factor * inv_diff, (rows, 128))
            off = jnp.broadcast_to(factor * inv_all, (rows, 128))
            g = e_ref[j].astype(f32) * jnp.where(positive_of(j), wide(on), wide(off))
            acc = acc + lax.dot_general(g.astype(bf16), bank_ref[pl.ds(j * tile, tile), :], NN, preferred_element_type=f32)
        finish((lse_all - lse_pos) * LN2, acc)

    @pl.when(jnp.logical_not(safe))
    def _():
        def pos_top(j, best):
            masked = jnp.where(positive_of(j), scores(j) * c, -1e30)
            return jnp.maximum(best, jnp.max(masked, axis=1, keepdims=True))
        top_pos = lax.fori_loop(0, tiles, pos_top, jnp.full((rows, 1), -1e30, f32))

        def pos_sum(j, total_pos):
            x = jnp.where(positive_of(j), scores(j) * c, -1e30)
            return total_pos + jnp.sum(jnp.exp2(x - top_pos), axis=1, keepdims=True)
        lse_pos = top_pos + jnp.log2(lax.fori_loop(0, tiles, pos_sum, jnp.zeros((rows, 1), f32)))
        cut_all = jnp.where(live, lse_all, 1e30)
        cut_pos = jnp.where(live, lse_pos, 1e30)

        def pull(j, acc):
            s = scores(j) * c
            g = jnp.exp2(s - cut_all) - jnp.exp2(jnp.where(positive_of(j), s, -1e30) - cut_pos)
            return acc + lax.dot_general(g.astype(bf16), bank_ref[pl.ds(j * tile, tile), :], NN, preferred_element_type=f32)
        finish((lse_all - lse_pos) * LN2, lax.fori_loop(0, tiles, pull, jnp.zeros((rows, width), f32)))

def bank_call(lengths, q, gold, target, labels, bank, *, rows=512, tile=1024, edt=bf16):
    length, width = q.shape
    slots = bank.shape[0]
    tiles = slots // tile
    docs = lengths.shape[1]
    return pl.pallas_call(
        functools.partial(bank_kernel, rows=rows, tile=tile, docs=docs),
        grid=(length // rows,),
        in_specs=[
            pl.BlockSpec(memory_space=pltpu.SMEM),
            pl.BlockSpec((rows, width), lambda i: (i, 0)),
            pl.BlockSpec((1, rows), lambda i: (0, i)),
            pl.BlockSpec((1, rows), lambda i: (0, i)),
            pl.BlockSpec((tiles, 1, tile), lambda i: (0, 0, 0)),
            pl.BlockSpec(memory_space=pl.ANY),
        ],
        out_specs=[
            pl.BlockSpec((rows, width), lambda i: (i, 0)),
            pl.BlockSpec((1, rows), lambda i: (0, i)),
            pl.BlockSpec((1, width), lambda i: (0, 0)),
        ],
        out_shape=[
            jax.ShapeDtypeStruct((length, width), f32),
            jax.ShapeDtypeStruct((1, length), f32),
            jax.ShapeDtypeStruct((1, width), f32),
        ],
        scratch_shapes=[
            pltpu.VMEM((slots, width), bf16),
            pltpu.VMEM((rows, tile), f32),
            pltpu.VMEM((rows, tile), f32),
            pltpu.VMEM((tiles, rows, tile), edt),
            pltpu.VMEM((tiles, rows, 1), f32),
            pltpu.SemaphoreType.DMA((tiles,)),
        ],
        compiler_params=pltpu.CompilerParams(vmem_limit_bytes=56 * 2 ** 20),
        name="bank",
    )(lengths, q, gold.reshape(1, length), target.reshape(1, length), labels.reshape(tiles, 1, tile), bank)

TN = (((0,), (0,)), ((), ()))
BIG = 1e30
STAT = 120
NEG = -1e30

def doc_bounds(lengths_ref, docs):
    lane = lax.broadcasted_iota(jnp.int32, (1, 128), 1)
    begin = jnp.zeros((1, 128), jnp.int32)
    end = jnp.zeros((1, 128), jnp.int32)
    at = jnp.int32(0)
    for j in range(docs):
        begin = jnp.where(lane == j, at, begin)
        at = at + lengths_ref[0, j]
        end = jnp.where(lane == j, at, end)
    begin = jnp.where(lane == docs, at, begin)
    end = jnp.where(lane == docs, 2 ** 30, end)
    return begin, end, at

def one_hot_docs(lengths_ref, docs, length):
    begin, end, _ = doc_bounds(lengths_ref, docs)
    place = lax.broadcasted_iota(jnp.int32, (length, 128), 0)
    return (place >= begin) & (place < end)

def split3(col):
    hi = col.astype(bf16).astype(f32)
    mid = (col - hi).astype(bf16).astype(f32)
    lo = col - hi - mid
    return hi, mid, lo

def with_stat(base, col, lane):
    hi, mid, lo = split3(col)
    return jnp.where(lane == STAT, hi, jnp.where(lane == STAT + 1, mid, jnp.where(lane == STAT + 2, lo, base))).astype(bf16)

def key_marks(hot, lane):
    ones = (lane >= STAT) & (lane < STAT + 3)
    return jnp.where(ones, 1.0, jnp.where(hot, 0.0, -BIG)).astype(bf16)

def attn_fwd_kernel(lengths_ref, q_ref, k_ref, v_ref, mixed_ref, lse_ref, aug_q, aug_k, kk, *, docs, dim, block):
    pair = pl.program_id(0)
    length = q_ref.shape[0]
    lane = lax.broadcasted_iota(jnp.int32, (1, 128), 1)

    @pl.when(pair == 0)
    def _():
        hot = one_hot_docs(lengths_ref, docs, length)
        marks = lane < docs + 1
        aug_q[...] = jnp.where(hot & marks, 1.0, 0.0).astype(bf16)
        aug_k[...] = key_marks(hot, lane)
        lse_ref[...] = jnp.zeros_like(lse_ref)

    kk[:, :128] = k_ref[...]
    kk[:, 128:] = aug_k[...]
    scale = 1.0 / math.sqrt(dim)
    first = lane < dim
    row = lax.broadcasted_iota(jnp.int32, (block, block), 0)
    col = lax.broadcasted_iota(jnp.int32, (block, block), 1)
    causal = row >= col
    for b in range(length // block):
        rows = pl.ds(b * block, block)
        q2 = q_ref[rows, :].astype(f32) * scale
        outs, lses = [], []
        for h in range(2):
            mine = first if h == 0 else jnp.logical_not(first)
            qq = jnp.concatenate([jnp.where(mine, q2, 0.0).astype(bf16), aug_q[rows, :]], axis=1)
            s_diag = lax.dot_general(qq, kk[rows, :], NT, preferred_element_type=f32)
            s_diag = jnp.where(causal, s_diag, NEG)
            top = jnp.max(s_diag, axis=1, keepdims=True)
            if b > 0:
                s_old = lax.dot_general(qq, kk[:b * block, :], NT, preferred_element_type=f32)
                top = jnp.maximum(top, jnp.max(s_old, axis=1, keepdims=True))
            e = jnp.exp(s_diag - top)
            total = jnp.sum(e, axis=1, keepdims=True)
            o = lax.dot_general(e.astype(bf16), v_ref[rows, :], NN, preferred_element_type=f32)
            if b > 0:
                e = jnp.exp(s_old - top)
                total = total + jnp.sum(e, axis=1, keepdims=True)
                o = o + lax.dot_general(e.astype(bf16), v_ref[:b * block, :], NN, preferred_element_type=f32)
            outs.append(o * (1.0 / total))
            lses.append(top + jnp.log(total))
        mixed_ref[rows, :] = jnp.where(first, outs[0], outs[1]).astype(bf16)
        lse_ref[rows, :] = jnp.where(lane == 2 * pair, lses[0], jnp.where(lane == 2 * pair + 1, lses[1], lse_ref[rows, :]))

def attn_fwd(lengths, projected, *, dim=64, block=256):
    length, width3 = projected.shape
    width = width3 // 3
    docs = lengths.shape[1]
    pairs = width // 128
    col = lambda off: pl.BlockSpec((length, 128), lambda p: (0, p + off))
    return pl.pallas_call(
        functools.partial(attn_fwd_kernel, docs=docs, dim=dim, block=block),
        grid=(pairs,),
        in_specs=[pl.BlockSpec(memory_space=pltpu.SMEM), col(0), col(pairs), col(2 * pairs)],
        out_specs=[col(0), pl.BlockSpec((length, 128), lambda p: (0, 0))],
        out_shape=[jax.ShapeDtypeStruct((length, width), bf16), jax.ShapeDtypeStruct((length, 128), f32)],
        scratch_shapes=[pltpu.VMEM((length, 128), bf16), pltpu.VMEM((length, 128), bf16), pltpu.VMEM((length, 256), bf16)],
        compiler_params=pltpu.CompilerParams(vmem_limit_bytes=48 * 2 ** 20),
        name="attend",
    )(lengths, projected, projected, projected)

def attn_bwd_kernel(lengths_ref, q_ref, k_ref, v_ref, mixed_ref, gmix_ref, lse_ref, dq_ref, dk_ref, dv_ref,
                    aug_q, aug_k, kk, vv, qq, gg, kt, dqt, *, docs, dim, block):
    pair = pl.program_id(0)
    length = q_ref.shape[0]
    blocks = length // block
    lane = lax.broadcasted_iota(jnp.int32, (1, 128), 1)

    @pl.when(pair == 0)
    def _():
        hot = one_hot_docs(lengths_ref, docs, length)
        marks = lane < docs + 1
        aug_q[...] = jnp.where(hot & marks, 1.0, 0.0).astype(bf16)
        aug_k[...] = key_marks(hot, lane)

    kk[:, :128] = k_ref[...]
    kk[:, 128:] = aug_k[...]
    vv[:, :128] = v_ref[...]
    vv[:, 128:] = aug_k[...]
    kt[...] = jnp.transpose(k_ref[...])
    scale = 1.0 / math.sqrt(dim)
    first = lane < dim
    q2 = q_ref[...].astype(f32) * scale
    g2 = gmix_ref[...].astype(f32)
    dots = g2 * mixed_ref[...].astype(f32)
    lse_all = lse_ref[...]
    marks_q = aug_q[...].astype(f32)
    for h in range(2):
        mine = first if h == 0 else jnp.logical_not(first)
        lse = jnp.sum(jnp.where(lane == 2 * pair + h, lse_all, 0.0), axis=1, keepdims=True)
        qq[h, :, :128] = jnp.where(mine, q2, 0.0).astype(bf16)
        qq[h, :, 128:] = with_stat(marks_q, -lse, lane)
        delta = jnp.sum(jnp.where(mine, dots, 0.0), axis=1, keepdims=True)
        gg[h, :, :128] = jnp.where(mine, g2, 0.0).astype(bf16)
        gg[h, :, 128:] = with_stat(jnp.zeros_like(marks_q), -delta, lane)
    krow = lax.broadcasted_iota(jnp.int32, (block, block), 0)
    qcol = lax.broadcasted_iota(jnp.int32, (block, block), 1)
    causal = qcol >= krow
    for kb in range(blocks):
        keys = pl.ds(kb * block, block)
        dk = jnp.zeros((block, 128), f32)
        dv = jnp.zeros((block, 128), f32)
        for h in range(2):
            for qb in range(kb, blocks):
                queries = pl.ds(qb * block, block)
                s = lax.dot_general(kk[keys, :], qq[h, queries, :], NT, preferred_element_type=f32)
                if qb == kb:
                    s = jnp.where(causal, s, NEG)
                p = jnp.exp(s)
                dp = lax.dot_general(vv[keys, :], gg[h, queries, :], NT, preferred_element_type=f32)
                ds = (p * dp).astype(bf16)
                dv = dv + lax.dot_general(p.astype(bf16), gg[h, queries, :128], NN, preferred_element_type=f32)
                dk = dk + lax.dot_general(ds, qq[h, queries, :128], NN, preferred_element_type=f32)
                part = lax.dot_general(kt[h * dim:(h + 1) * dim, keys], ds, NN, preferred_element_type=f32)
                if kb == 0:
                    dqt[h * dim:(h + 1) * dim, queries] = part
                else:
                    dqt[h * dim:(h + 1) * dim, queries] += part
        dk_ref[keys, :] = dk.astype(bf16)
        dv_ref[keys, :] = dv.astype(bf16)
    dq_ref[...] = (jnp.transpose(dqt[...]) * scale).astype(bf16)

def attn_bwd(lengths, projected, mixed, gmix, lse, *, dim=64, block=256):
    length, width3 = projected.shape
    width = width3 // 3
    docs = lengths.shape[1]
    pairs = width // 128
    col = lambda off: pl.BlockSpec((length, 128), lambda p: (0, p + off))
    one = jax.ShapeDtypeStruct((length, width), bf16)
    return pl.pallas_call(
        functools.partial(attn_bwd_kernel, docs=docs, dim=dim, block=block),
        grid=(pairs,),
        in_specs=[pl.BlockSpec(memory_space=pltpu.SMEM), col(0), col(pairs), col(2 * pairs), col(0), col(0),
                  pl.BlockSpec((length, 128), lambda p: (0, 0))],
        out_specs=[col(0), col(0), col(0)],
        out_shape=[one, one, one],
        scratch_shapes=[pltpu.VMEM((length, 128), bf16), pltpu.VMEM((length, 128), bf16),
                        pltpu.VMEM((length, 256), bf16), pltpu.VMEM((length, 256), bf16),
                        pltpu.VMEM((2, length, 256), bf16), pltpu.VMEM((2, length, 256), bf16),
                        pltpu.VMEM((128, length), bf16), pltpu.VMEM((128, length), f32)],
        compiler_params=pltpu.CompilerParams(vmem_limit_bytes=48 * 2 ** 20),
        name="attend_back",
    )(lengths, projected, projected, projected, mixed, gmix, lse)


def place_tables(length, width):
    freq = np.exp(np.arange(width // 2, dtype=np.float64) * (-2.0 * math.log(10000.0) / width))
    angles = np.arange(length, dtype=np.float64)[:, None] * freq[None, :]
    return (np.concatenate([np.sin(angles), np.cos(angles)], axis=1).astype(np.float32),
            freq.astype(np.float32)[None, :])

def norm_stats(v):
    center = v - jnp.mean(v, axis=1, keepdims=True)
    inv = lax.rsqrt(jnp.mean(center * center, axis=1, keepdims=True) + 1e-5)
    return center * inv, inv

def front_kernel(lengths_ref, x_ref, table_ref, freq_ref, gain_ref, bias_ref, w_ref,
                 stream_ref, normed_ref, proj_ref, starts, *, docs):
    step = pl.program_id(0)
    rows, width = x_ref.shape
    half = width // 2
    begin, end, _ = doc_bounds(lengths_ref, docs)

    @pl.when(step == 0)
    def _():
        at = jnp.transpose(jnp.broadcast_to(begin.astype(f32), (128, 128)))[:, :1]
        angle = at * freq_ref[...]
        both = jnp.concatenate([jnp.sin(angle), jnp.cos(angle)], axis=1)
        hi = both.astype(bf16)
        mid = (both - hi.astype(f32)).astype(bf16)
        starts[:128, :] = hi
        starts[128:256, :] = mid
        starts[256:, :] = (both - hi.astype(f32) - mid.astype(f32)).astype(bf16)

    place = step * rows + lax.broadcasted_iota(jnp.int32, (rows, 128), 0)
    hot = jnp.where((place >= begin) & (place < end), 1.0, 0.0).astype(bf16)
    start = lax.dot_general(jnp.concatenate([hot, hot, hot], axis=1), starts[...], NN, preferred_element_type=f32)
    sin_b, cos_b = start[:, :half], start[:, half:]
    sin_t, cos_t = table_ref[:, :half], table_ref[:, half:]
    x = x_ref[...].astype(f32)
    stream = jnp.concatenate([x[:, :half] + (sin_t * cos_b - cos_t * sin_b),
                              x[:, half:] + (cos_t * cos_b + sin_t * sin_b)], axis=1)
    stream_ref[...] = stream
    unit, _ = norm_stats(stream)
    normed = (unit * gain_ref[...] + bias_ref[...]).astype(bf16)
    normed_ref[...] = normed
    proj_ref[...] = lax.dot_general(normed, w_ref[...], NN, preferred_element_type=f32).astype(bf16)

def front(lengths, x, gain, bias, w, *, rows=256):
    length, width = x.shape
    table, freq = place_tables(length, width)
    docs = lengths.shape[1]
    blk = pl.BlockSpec((rows, width), lambda i: (i, 0))
    whole = lambda a: pl.BlockSpec(a.shape, lambda i: (0,) * a.ndim)
    return pl.pallas_call(
        functools.partial(front_kernel, docs=docs),
        grid=(length // rows,),
        in_specs=[pl.BlockSpec(memory_space=pltpu.SMEM), blk, blk, whole(freq), whole(gain), whole(bias), whole(w)],
        out_specs=[blk, blk, pl.BlockSpec((rows, w.shape[1]), lambda i: (i, 0))],
        out_shape=[jax.ShapeDtypeStruct((length, width), f32), jax.ShapeDtypeStruct((length, width), bf16),
                   jax.ShapeDtypeStruct((length, w.shape[1]), bf16)],
        scratch_shapes=[pltpu.VMEM((384, width), bf16)],
        compiler_params=pltpu.CompilerParams(vmem_limit_bytes=40 * 2 ** 20),
        name="front",
    )(lengths, x, table, freq, gain, bias, w)

ERF = (0.254829592, -0.284496736, 1.421413741, -1.453152027, 1.061405429)
ERF_P = 0.3275911

def gelu_both(h):
    bell = jnp.exp(h * h * -0.5)
    t = 1.0 / (1.0 + jnp.abs(h) * (ERF_P / math.sqrt(2.0)))
    poly = t * (ERF[0] + t * (ERF[1] + t * (ERF[2] + t * (ERF[3] + t * ERF[4]))))
    tail = 0.5 * poly * bell
    phi = jnp.where(h < 0.0, tail, 1.0 - tail)
    return h * phi, phi + h * bell * (1.0 / math.sqrt(2.0 * math.pi))

def ffn_kernel(stream_ref, mixed_ref, w_out_ref, b_out_ref, gain_ref, bias_ref, w_up_ref, b_up_ref, w_down_ref, b_down_ref,
               after_ref, normed_ref, act_ref, slope_ref, out_ref, *, chunk):
    after = stream_ref[...] + lax.dot_general(mixed_ref[...], w_out_ref[...], NN, preferred_element_type=f32) + b_out_ref[...]
    after_ref[...] = after
    unit, _ = norm_stats(after)
    normed = (unit * gain_ref[...] + bias_ref[...]).astype(bf16)
    normed_ref[...] = normed
    acc = after + b_down_ref[...]
    wide = w_up_ref.shape[1]
    for c in range(wide // chunk):
        cols = pl.ds(c * chunk, chunk)
        hidden = lax.dot_general(normed, w_up_ref[:, cols], NN, preferred_element_type=f32) + b_up_ref[:, cols]
        act, slope = gelu_both(hidden)
        act = act.astype(bf16)
        act_ref[:, cols] = act
        slope_ref[:, cols] = slope.astype(bf16)
        acc = acc + lax.dot_general(act, w_down_ref[cols, :], NN, preferred_element_type=f32)
    out_ref[...] = acc.astype(bf16)

def ffn(stream, mixed, w_out, b_out, gain, bias, w_up, b_up, w_down, b_down, *, rows=256, chunk=512):
    length, width = stream.shape
    wide = w_up.shape[1]
    blk = pl.BlockSpec((rows, width), lambda i: (i, 0))
    big = pl.BlockSpec((rows, wide), lambda i: (i, 0))
    whole = lambda a: pl.BlockSpec(a.shape, lambda i: (0,) * a.ndim)
    args = (w_out, b_out, gain, bias, w_up, b_up, w_down, b_down)
    return pl.pallas_call(
        functools.partial(ffn_kernel, chunk=chunk),
        grid=(length // rows,),
        in_specs=[blk, blk] + [whole(a) for a in args],
        out_specs=[blk, blk, big, big, blk],
        out_shape=[jax.ShapeDtypeStruct((length, width), f32), jax.ShapeDtypeStruct((length, width), bf16),
                   jax.ShapeDtypeStruct((length, wide), bf16), jax.ShapeDtypeStruct((length, wide), bf16),
                   jax.ShapeDtypeStruct((length, width), bf16)],
        compiler_params=pltpu.CompilerParams(vmem_limit_bytes=48 * 2 ** 20),
        name="ffn",
    )(stream, mixed, *args)

def norm_back(g, gain, unit, inv):
    gu = g * gain
    return inv * (gu - jnp.mean(gu, axis=1, keepdims=True) - unit * jnp.mean(gu * unit, axis=1, keepdims=True))

def colsum(x):
    return jnp.sum(x, axis=0, keepdims=True)

def permuted_rows(dst, src, me, chunk):
    for a in range(src.shape[0] // chunk):
        dst[pl.ds(pl.multiple_of(lax.bitwise_xor(jnp.int32(a), me) * chunk, chunk), chunk), :] = src[a * chunk:(a + 1) * chunk, :]

def down_grad_kernel(me_ref, act_ref, g_ref, send_ref, keep_ref, g_low):
    i = pl.program_id(0)

    @pl.when(i == 0)
    def _():
        g_low[...] = g_ref[...].astype(bf16)
    out = lax.dot_general(act_ref[...], g_low[...], TN, preferred_element_type=f32).astype(bf16)

    @pl.when(i < 8)
    def _():
        send_ref[...] = out

    @pl.when(i >= 8)
    def _():
        keep_ref[...] = out

def down_grad(me, act, g):
    length, width = g.shape
    wide = act.shape[1]
    block = wide // 16

    def act_index(i, me_ref):
        keep, ab, pq = i // 8, (i // 4) % 2, i % 4
        core = jnp.bitwise_xor(1 - keep, me_ref[0])
        return (0, ab * 8 + core * 4 + jnp.bitwise_xor(pq, jnp.where(ab == 0, me_ref[1], me_ref[2])))
    return pl.pallas_call(
        down_grad_kernel,
        grid_spec=pltpu.PrefetchScalarGridSpec(
            num_scalar_prefetch=1, grid=(16,),
            in_specs=[pl.BlockSpec((length, block), act_index), pl.BlockSpec((length, width), lambda i, m: (0, 0))],
            out_specs=[pl.BlockSpec((block, width), lambda i, m: (jnp.minimum(i, 7), 0)),
                       pl.BlockSpec((block, width), lambda i, m: (jnp.maximum(i - 8, 0), 0))],
            scratch_shapes=[pltpu.VMEM((length, width), bf16)]),
        out_shape=[jax.ShapeDtypeStruct((wide // 2, width), bf16)] * 2,
        compiler_params=pltpu.CompilerParams(vmem_limit_bytes=40 * 2 ** 20),
        name="down_grad",
    )(me, act, g)

def ffn_back_kernel(me_ref, g_ref, slope_ref, w_down_ref, w_up_ref, normed_ref, after_ref, gain_ref, mixed_ref, w_out_ref,
                    bdown_ref, up_send, up_keep, gafter_ref, gmix_ref, out_send, out_keep, small_ref,
                    g_low, norm_t, acc, bup):
    i = pl.program_id(0)
    steps = pl.num_programs(0)
    width = g_ref.shape[1]
    tile = slope_ref.shape[1]
    row8 = width // 8

    def arranged(t, dst):
        for ab in range(2):
            for a in range(8):
                r = lax.bitwise_xor(jnp.int32(a), me_ref[0] * 4 + me_ref[1 + ab])
                dst[ab, pl.ds(pl.multiple_of(r * row8, row8), row8), :] = t[a * row8:(a + 1) * row8, :]

    @pl.when(i == 0)
    def _():
        g_low[...] = g_ref[...].astype(bf16)
        arranged(jnp.transpose(normed_ref[...]), norm_t)
        acc[...] = jnp.zeros_like(acc)
    gh = lax.dot_general(g_low[...], w_down_ref[...], NT, preferred_element_type=f32) * slope_ref[...].astype(f32)
    bup[pl.ds(i, 1), :] = colsum(gh)
    gh = gh.astype(bf16)
    acc[...] += lax.dot_general(gh, w_up_ref[...], NT, preferred_element_type=f32)
    lhs = norm_t[i // (steps // 2)]
    grad = lax.dot_general(lhs, gh, NN, preferred_element_type=f32).astype(bf16)
    up_keep[...] = grad[:width // 2, :]
    up_send[...] = grad[width // 2:, :]

    @pl.when(i == steps - 1)
    def _():
        unit, inv = norm_stats(after_ref[...])
        gn = acc[...]
        ga = g_ref[...] + norm_back(gn, gain_ref[...], unit, inv)
        gafter_ref[...] = ga
        low = ga.astype(bf16)
        gmix_ref[...] = lax.dot_general(low, w_out_ref[...], NT, preferred_element_type=f32).astype(bf16)
        arranged(jnp.transpose(mixed_ref[...]), norm_t)
        for ab in range(2):
            cols = slice(ab * width // 2, (ab + 1) * width // 2)
            grad_out = lax.dot_general(norm_t[ab], low[:, cols], NN, preferred_element_type=f32).astype(bf16)
            out_keep[:, cols] = grad_out[:width // 2, :]
            out_send[:, cols] = grad_out[width // 2:, :]
        small_ref[0:1, :] = bdown_ref[...]
        small_ref[1:2, :] = colsum(gn * unit)
        small_ref[2:3, :] = colsum(gn)
        small_ref[3:4, :] = colsum(ga)
        per = width // tile
        for k in range(steps // per):
            for m in range(per):
                small_ref[4 + k:5 + k, m * tile:(m + 1) * tile] = bup[k * per + m:k * per + m + 1, :]

def ffn_back(me, g, slope, w_down, w_up, normed, after, gain, mixed, w_out, bdown, *, tile=256):
    length, width = g.shape
    wide = slope.shape[1]
    steps = wide // tile
    whole = lambda a: pl.BlockSpec(a.shape, lambda i, m: (0,) * a.ndim)
    full = lambda s: pl.BlockSpec(s, lambda i, m: (0,) * len(s))
    half = pl.BlockSpec((width // 2, tile), lambda i, m: (0, i))
    small_rows = 4 + wide // width
    return pl.pallas_call(
        ffn_back_kernel,
        grid_spec=pltpu.PrefetchScalarGridSpec(
            num_scalar_prefetch=1, grid=(steps,),
            in_specs=[whole(g), pl.BlockSpec((length, tile), lambda i, m: (0, i)), pl.BlockSpec((tile, width), lambda i, m: (i, 0)),
                      pl.BlockSpec((width, tile), lambda i, m: (0, i)), whole(normed), whole(after), whole(gain), whole(mixed),
                      whole(w_out), whole(bdown)],
            out_specs=[half, half, full((length, width)), full((length, width)), full((width // 2, width)), full((width // 2, width)),
                       full((small_rows, width))],
            scratch_shapes=[pltpu.VMEM((length, width), bf16), pltpu.VMEM((2, width, length), bf16), pltpu.VMEM((length, width), f32),
                            pltpu.VMEM((steps, tile), f32)]),
        out_shape=[jax.ShapeDtypeStruct((width // 2, wide), bf16)] * 2
        + [jax.ShapeDtypeStruct((length, width), f32), jax.ShapeDtypeStruct((length, width), bf16)]
        + [jax.ShapeDtypeStruct((width // 2, width), bf16)] * 2 + [jax.ShapeDtypeStruct((small_rows, width), f32)],
        compiler_params=pltpu.CompilerParams(vmem_limit_bytes=56 * 2 ** 20),
        name="ffn_back",
    )(me, g, slope, w_down, w_up, normed, after, gain, mixed, w_out, bdown)

def qkv_grad_kernel(me_ref, gp_q, gp_k, gp_v, normed_ref, send_ref, keep_ref, norm_t):
    width = normed_ref.shape[1]
    row8 = width // 8
    t = jnp.transpose(normed_ref[...])
    for ab in range(2):
        for a in range(8):
            r = lax.bitwise_xor(jnp.int32(a), me_ref[0] * 4 + me_ref[1 + ab])
            norm_t[ab, pl.ds(pl.multiple_of(r * row8, row8), row8), :] = t[a * row8:(a + 1) * row8, :]
    at = 0
    cut = 3 * width // 2
    for part in (gp_q, gp_k, gp_v):
        for c in range(0, width, 256):
            ab = 0 if at < cut else 1
            grad = lax.dot_general(norm_t[ab], part[:, c:c + 256], NN, preferred_element_type=f32).astype(bf16)
            keep_ref[:, at:at + 256] = grad[:width // 2, :]
            send_ref[:, at:at + 256] = grad[width // 2:, :]
            at += 256

def qkv_grad(me, gq, gk, gv, normed):
    length, width = normed.shape
    vm = pl.BlockSpec(memory_space=pltpu.VMEM)
    return pl.pallas_call(
        qkv_grad_kernel,
        in_specs=[pl.BlockSpec(memory_space=pltpu.SMEM), vm, vm, vm, vm],
        out_specs=[vm, vm],
        out_shape=[jax.ShapeDtypeStruct((width // 2, 3 * width), bf16)] * 2,
        scratch_shapes=[pltpu.VMEM((2, width, length), bf16)],
        compiler_params=pltpu.CompilerParams(vmem_limit_bytes=48 * 2 ** 20),
        name="qkv_grad",
    )(me, gq, gk, gv, normed)

def front_back_kernel(gq, gk, gv, w_ref, stream_ref, gafter_ref, gain_ref, out_ref, small_ref):
    i = pl.program_id(0)
    width = stream_ref.shape[1]
    gn = lax.dot_general(gq[...], w_ref[:, :width], NT, preferred_element_type=f32)
    gn = gn + lax.dot_general(gk[...], w_ref[:, width:2 * width], NT, preferred_element_type=f32)
    gn = gn + lax.dot_general(gv[...], w_ref[:, 2 * width:], NT, preferred_element_type=f32)
    unit, inv = norm_stats(stream_ref[...])
    out_ref[...] = (gafter_ref[...] + norm_back(gn, gain_ref[...], unit, inv)).astype(bf16)
    part = jnp.concatenate([colsum(gn * unit), colsum(gn)], axis=0)
    small_ref[...] = jnp.where(i == 0, part, small_ref[...] + part)

def front_back(gq, gk, gv, w, stream, gafter, gain, *, rows=256):
    length, width = stream.shape
    blk = pl.BlockSpec((rows, width), lambda i: (i, 0))
    whole = lambda a: pl.BlockSpec(a.shape, lambda i: (0,) * a.ndim)
    return pl.pallas_call(
        front_back_kernel,
        grid=(length // rows,),
        in_specs=[blk, blk, blk, whole(w), blk, blk, whole(gain)],
        out_specs=[blk, pl.BlockSpec((2, width), lambda i: (0, 0))],
        out_shape=[jax.ShapeDtypeStruct((length, width), bf16), jax.ShapeDtypeStruct((2, width), f32)],
        compiler_params=pltpu.CompilerParams(vmem_limit_bytes=40 * 2 ** 20),
        name="front_back",
    )(gq, gk, gv, w, stream, gafter, gain)


def finish_kernel(me_ref, own_a, own_b, got_a, got_b, out_ref, *, by_rows, nt, n):
    i = pl.program_id(0)
    rows = own_a.shape[0]
    chunk = rows // (4 * n)

    def lay(ab, own, got):
        for near, ref in ((0, own), (1, got)):
            core = lax.bitwise_xor(jnp.int32(near), me_ref[0])
            for pq in range(4):
                for z in range(n):
                    at = core * 4 + lax.bitwise_xor(jnp.int32(pq), me_ref[1 + ab])
                    at = at * n + lax.bitwise_xor(jnp.int32(z), me_ref[3])
                    at = at * chunk + (ab * 2 * rows if by_rows else 0)
                    r = (pq * n + z) * chunk
                    out_ref[pl.ds(pl.multiple_of(at, chunk), chunk), :] = ref[r:r + chunk, :].astype(f32)
    if by_rows:
        lay(0, own_a, got_a)
        lay(1, own_b, got_b)
    else:
        @pl.when(i < nt)
        def _():
            lay(0, own_a, got_a)

        @pl.when(i >= nt)
        def _():
            lay(1, own_b, got_b)

def finish(me, own_a, own_b, got_a, got_b, *, by_rows, n, tile):
    rows, width = own_a.shape
    nt = width // tile
    if by_rows:
        spec_a = spec_b = pl.BlockSpec((rows, tile), lambda i, m: (0, i))
        grid, shape = nt, (4 * rows, width)
    else:
        spec_a = pl.BlockSpec((rows, tile), lambda i, m: (0, jnp.minimum(i, nt - 1)))
        spec_b = pl.BlockSpec((rows, tile), lambda i, m: (0, jnp.maximum(i - nt, 0)))
        grid, shape = 2 * nt, (2 * rows, 2 * width)
    return pl.pallas_call(
        functools.partial(finish_kernel, by_rows=by_rows, nt=nt, n=n),
        grid_spec=pltpu.PrefetchScalarGridSpec(
            num_scalar_prefetch=1, grid=(grid,),
            in_specs=[spec_a, spec_b, spec_a, spec_b],
            out_specs=pl.BlockSpec((shape[0], tile), lambda i, m: (0, i))),
        out_shape=jax.ShapeDtypeStruct(shape, f32),
        compiler_params=pltpu.CompilerParams(vmem_limit_bytes=40 * 2 ** 20),
        name="finish",
    )(me, own_a, own_b, got_a, got_b)

class Links:
    def __init__(self, mesh):
        self.sizes = dict(mesh.shape)
        self.n = self.sizes["rows"] // 2

    def swap(self, x, axis, bit):
        return lax.ppermute(x, axis, [(a, a ^ bit) for a in range(self.sizes[axis])])

    def core(self, x):
        return self.swap(x, "bank", 1)

    def near(self, x):
        return self.swap(x, "bank", 2)

    def side(self, x):
        return self.swap(x, "rows", 1)

def plus(*terms):
    out = terms[0].astype(f32)
    for t in terms[1:]:
        out = out + t.astype(f32)
    return out.astype(bf16)

def total(links, me, send, keep, *, by_rows, tile):
    n = links.n
    got = links.core(send)
    rows, width = keep.shape
    if by_rows:
        cut = lambda x: (x[:rows // 2], x[rows // 2:])
    else:
        cut = lambda x: (x[:, :width // 2], x[:, width // 2:])
    (ka, kb), (ga, gb) = cut(keep), cut(got)
    half = ka.shape[0] // 2
    sa, sb = plus(ka[half:], ga[half:]), plus(kb[half:], gb[half:])
    ra, rb = links.near(sa), links.side(sb)
    a, b = plus(ka[:half], ga[:half]), plus(kb[:half], gb[:half])
    half //= 2
    sa, sb = plus(a[half:], ra[half:]), plus(b[half:], rb[half:])
    a, b = plus(a[:half], ra[:half]), plus(b[:half], rb[:half])
    ra, rb = links.side(sa), links.near(sb)
    a, b = plus(a, ra), plus(b, rb)
    chunk = half // n
    w = a.shape[1]
    fine = half % (n * 16) == 0 and n & (n - 1) == 0
    if fine:
        zi = lax.axis_index("rows") // 2
        piece = lambda k: jnp.stack([lax.dynamic_slice(v, ((zi ^ k) * chunk, 0), (chunk, w)) for v in (a, b)])
        got = [links.swap(piece(k), "rows", 2 * k) for k in range(1, n)]
        mine = plus(piece(0), *got)
        got = [links.swap(mine, "rows", 2 * k) for k in range(1, n)]
        a = jnp.concatenate([mine[0]] + [g[0] for g in got], axis=0)
        b = jnp.concatenate([mine[1]] + [g[1] for g in got], axis=0)
    else:
        groups = [[r for r in range(2 * n) if r % 2 == y] for y in range(2)]
        a, b = lax.psum((a, b), "rows", axis_index_groups=groups)
    ra, rb = links.side(a), links.near(b)
    a, b = jnp.concatenate([a, ra], axis=0), jnp.concatenate([b, rb], axis=0)
    ra, rb = links.near(a), links.side(b)
    a, b = jnp.concatenate([a, ra], axis=0), jnp.concatenate([b, rb], axis=0)
    ga, gb = links.core(a), links.core(b)
    return finish(me, a, b, ga, gb, by_rows=by_rows, n=n if fine else 1, tile=tile)

def total_small(links, x):
    for axis in ("bank", "rows"):
        bit = 1
        while bit < links.sizes[axis]:
            x = x + links.swap(x, axis, bit)
            bit *= 2
    return x

def body(mesh, hidden_in, lengths, ln1_gain, ln1_bias, w_qkv, w_out, b_out, ln2_gain, ln2_bias, w_up, b_up, w_down, b_down,
         bank, bank_labels, target_slots, gold_ids):
    links = Links(mesh)
    row = lambda v: v.reshape(1, -1)
    width = hidden_in.shape[1]
    ib, ir = lax.axis_index("bank"), lax.axis_index("rows")
    core, x, y = ib % 2, ib // 2, ir % 2
    me = jnp.stack([core, x * 2 + y, y * 2 + x, ir // 2 if (links.n & (links.n - 1)) == 0 else 0]).astype(jnp.int32)
    bank_all = lax.all_gather(bank, "bank", axis=0, tiled=True)
    labels_all = lax.all_gather(bank_labels, "bank", axis=0, tiled=True)
    stream, normed_a, projected = front(lengths, hidden_in, row(ln1_gain), row(ln1_bias), w_qkv)
    mixed, lse = attn_fwd(lengths, projected, block=512)
    after, normed_c, act, slope, block_out = ffn(stream, mixed, w_out, row(b_out), row(ln2_gain), row(ln2_bias), w_up, row(b_up),
                                                 w_down, row(b_down), chunk=256)
    g, loss, bdown = bank_call(lengths, block_out, gold_ids, target_slots, labels_all, bank_all, edt=f32)
    down_send, down_keep = down_grad(me, act, g)
    w_down_grad = total(links, me, down_send, down_keep, by_rows=True, tile=256)
    up_send, up_keep, gafter, gmix, out_send, out_keep, small = ffn_back(
        me, g, slope, w_down, w_up, normed_c, after, row(ln2_gain), mixed, w_out, bdown, tile=512)
    w_up_grad = total(links, me, up_send, up_keep, by_rows=False, tile=512)
    w_out_grad = total(links, me, out_send, out_keep, by_rows=False, tile=256)
    small = total_small(links, small)
    gq, gk, gv = attn_bwd(lengths, projected, mixed, gmix, lse, block=512)
    qkv_send, qkv_keep = qkv_grad(me, gq, gk, gv, normed_a)
    w_qkv_grad = total(links, me, qkv_send, qkv_keep, by_rows=False, tile=384)
    input_grad, small1 = front_back(gq, gk, gv, w_qkv, stream, gafter, row(ln1_gain))
    small1 = total_small(links, small1)
    return (block_out, loss.reshape(-1), input_grad, small1[0], small1[1], w_qkv_grad, w_out_grad, small[3], small[1], small[2],
            w_up_grad, small[4:].reshape(-1), w_down_grad, small[0])

def solution(mesh):
    in_specs = (
        P(("rows", "bank"), None),
        P(("rows", "bank"), None),
        P(),
        P(),
        P(),
        P(),
        P(),
        P(),
        P(),
        P(),
        P(),
        P(),
        P(),
        P("bank", None),
        P("bank"),
        P(("rows", "bank")),
        P(("rows", "bank")),
    )
    out_specs = (
        P(("rows", "bank"), None),
        P(("rows", "bank")),
        P(("rows", "bank"), None),
        P(),
        P(),
        P(),
        P(),
        P(),
        P(),
        P(),
        P(),
        P(),
        P(),
        P(),
    )
    return jax.shard_map(functools.partial(body, mesh), mesh=mesh, in_specs=in_specs, out_specs=out_specs, check_vma=False)
```

time: 583 us -> 381 us (0.65); the launches traced: 573 us -> 381 us
  matrix products: 214 us -> 0 us
  Pallas kernels: 0 us -> 147 us
  other arithmetic: 88.6 us -> 4.07 us
  starting transfers between devices: 0.08 us -> 75.3 us
  waiting for transfers between devices: 174 us -> 111 us
  blocking collectives: 49 us -> 6.61 us
  local copies, waits for them, and re-layouts: 32.8 us -> 21.1 us
    dot_general x62 -> x0, matrix products: 214 us -> none  [the longest x1 29.6 us: body(): jnp.dot(grad_scores, bank_all, preferred_element_type=jnp.float32)]
    psum x1 -> x0, waiting for transfers between devices: 174 us -> none  [body(): lax.psum((grad_w_qkv, grad_w_out, grad_b_out, grad_ln1_gain, grad_ln1_bia...]
    pallas_call x0 -> x13, Pallas kernels: none -> 147 us  [the longest x1 47.5 us: bank_call(): pl.pallas_call(functools.partial(bank_kernel, rows=rows, tile=tile, docs=...]
    ppermute x0 -> x78, waiting for transfers between devices: none -> 101 us  [swap(): lax.ppermute(x, axis, [(a, a ^ bit) for a in range(self.sizes[axis])])]
    ppermute x0 -> x78, starting transfers between devices: none -> 75.3 us  [swap(): lax.ppermute(x, axis, [(a, a ^ bit) for a in range(self.sizes[axis])])]
    psum x1 -> x0, blocking collectives: 42.8 us -> none  [body(): lax.psum((grad_w_qkv, grad_w_out, grad_b_out, grad_ln1_gain, grad_ln1_bia...]
    convert_element_type x11 -> x24, other arithmetic: 41.5 us -> 2.57 us  [plus(): return out.astype(bf16)]
    reduce_sum x16 -> x0, other arithmetic: 36.9 us -> none  [the longest x1 20.9 us: slot_stats(): jnp.sum(jnp.where(positive, jnp.exp(masked - top_pos[:, None]), 0.0), axi...]
  transfers between devices with their start and end apart: 2 -> 79, of which waited for: 1 -> 45; matrix products, arithmetic and copies ran while one was open for 14% -> 2% of each run, Pallas kernels for 0% -> 21%
where the time goes in v1:
time: 381 us
  Pallas kernels  147 us (39%)
  waiting for transfers between devices  111 us (29%)
  starting transfers between devices  75.3 us (20%)
  local copies, waits for them, and re-layouts  21.1 us (6%)
  between operations  15.3 us (4%)
  blocking collectives  6.61 us (2%)
  other arithmetic  4.07 us (1%)
    ppermute x78, waiting for transfers between devices, swap(): lax.ppermute(x, axis, [(a, a ^ bit) for a in range(self.sizes[axis])])  101 us
    ppermute x78, starting transfers between devices, swap(): lax.ppermute(x, axis, [(a, a ^ bit) for a in range(self.sizes[axis])])  75.3 us
    pallas_call x1, Pallas kernels, bank_call(): pl.pallas_call(functools.partial(bank_kernel, rows=rows, tile=tile, docs=...  47.5 us
    pallas_call x1, Pallas kernels, attn_bwd(): pl.pallas_call(functools.partial(attn_bwd_kernel, docs=docs, dim=dim, blo...  23.3 us
    unnamed x88, local copies, waits for them, and re-layouts  19.4 us
    pallas_call x1, Pallas kernels, ffn_back(): pl.pallas_call(ffn_back_kernel, grid_spec=pltpu.PrefetchScalarGridSpec(nu...  17.8 us
    pallas_call x1, Pallas kernels, ffn(): pl.pallas_call(functools.partial(ffn_kernel, chunk=chunk), grid=(length /...  15.3 us
    pallas_call x1, Pallas kernels, attn_fwd(): pl.pallas_call(functools.partial(attn_fwd_kernel, docs=docs, dim=dim, blo...  11.8 us
  transfers between devices with their start and end apart: 79, of which 45 were waited for; matrix products, arithmetic and copies ran while one was open for 2% of the time, Pallas kernels for 21%

profile of v1, /device:TPU:0, one launch (start us, length us, event | category | flops | bytes accessed | tf_op | source)
XLA Modules:
  0.0 380.5 jit_solution(4794570354748559404)
XLA Ops:
  12.2 5.5 %front.1 = (f32[1024,512]{1,0:T(8,128)S(1)}, bf16[1024,512]{1,0:T(8,128)(2,1)S(1)}, bf16[1024,1536]{1,0:T(8,128)(2,1)S(1)}) custom-call(s32[1,16]{1,0:T(1,128)S(1)} %copy-done.23, bf16[1024,512]{1,0:T(8,128)(2,1)S(1)} %copy-done.18, f32[1024,512]{1,0:T(8,128)S(1)} %copy-done.12, f32[1,256]{1,0:T(1,128)S(1)} %copy-done.31, f32[1,512]{1,0:T(1,128)S(1)} %bitcast.280, ...), custom_call_target="tpu_custom_call" | custom-call | tf_op jit(solution)/shard_map/front/pallas_call | solution.py:413
  20.2 11.8 %attend.1 = (bf16[1024,512]{1,0:T(8,128)(2,1)S(1)}, f32[1024,128]{1,0:T(8,128)S(1)}) custom-call(s32[1,16]{1,0:T(1,128)S(1)} %copy-done.23, bf16[1024,1536]{1,0:T(8,128)(2,1)S(1)} %get-tuple-element.44.q_ref.k_ref.v_ref, bf16[1024,1536]{1,0:T(8,128)(2,1)S(1)} %get-tuple-element.44.q_ref.k_ref.v_ref, bf16[1024,1536]{1,0:T(8,128)(2,1)S(1)} %get-tuple-element.44.q_ref.k_ref.v_ref), custom_call_target="tpu_custom_call" | custom-call | tf_op jit(solution)/shard_map/attend/pallas_call | solution.py:269
  36.0 15.3 %ffn.1 = (f32[1024,512]{1,0:T(8,128)S(1)}, bf16[1024,512]{1,0:T(8,128)(2,1)S(1)}, bf16[1024,2048]{1,0:T(8,128)(2,1)}, bf16[1024,2048]{1,0:T(8,128)(2,1)}, bf16[1024,512]{1,0:T(8,128)(2,1)}) custom-call(f32[1024,512]{1,0:T(8,128)} %copy-done.5, bf16[1024,512]{1,0:T(8,128)(2,1)S(1)} %copy-done.2, bf16[512,512]{1,0:T(8,128)(2,1)S(1)} %copy-done.13, ...), custom_call_target="tpu_custom_call" | custom-call | tf_op jit(solution)/shard_map/ffn/pallas_call | solution.py:462
  53.7 6.6 %all_gather.6 = s32[8192]{0:T(1024)} all-gather(s32[2048]{0:T(1024)S(1)} %copy-done.33), channel_id=1, replica_groups=mesh['rows'=8,'bank'=4] {'bank'}, dimensions={0}, use_global_device_ids=true | all-gather | bytes 40960 | tf_op jit(solution)/shard_map/all_gather | solution.py:785
  60.9 10.0 %all-gather.2.cloned.1.call-done.bank_hbm = bf16[8192,512]{1,0:T(8,128)(2,1)} async-done(((bf16[2048,512]{1,0:T(8,128)(2,1)}), bf16[8192,512]{1,0:T(8,128)(2,1)}) %all-gather.2.cloned.1.call-update) | async-done | bytes 8388624 | tf_op jit(solution)/shard_map/all_gather | solution.py:784
  70.8 47.5 %bank.1 = (f32[1024,512]{1,0:T(8,128)}, f32[1,1024]{1,0:T(1,128)}, f32[1,512]{1,0:T(1,128)}) custom-call(s32[1,16]{1,0:T(1,128)} %lengths_ref.7, bf16[1024,512]{1,0:T(8,128)(2,1)} %get-tuple-element.29.q_ref, s32[1,1024]{1,0:T(1,128)} %bitcast.291, s32[1,1024]{1,0:T(1,128)} %bitcast.292, s32[8,1,1024]{2,1,0:T(1,128)} %bitcast.289, ...), custom_call_target="tpu_custom_call" | custom-call | tf_op jit(solution)/shard_map/bank/pallas_call | solution.py:148
  118.3 17.8 %ffn_back.1 = (bf16[256,2048]{1,0:T(8,128)(2,1)}, bf16[256,2048]{1,0:T(8,128)(2,1)}, f32[1024,512]{1,0:T(8,128)}, bf16[1024,512]{1,0:T(8,128)(2,1)}, bf16[256,51...) custom-call(s32[4]{0:T(128)} %pad_add_fusion.me_ref, f32[1024,512]{1,0:T(8,128)} %get-tuple-element.48.g_ref, ...), custom_call_target="tpu_custom_call" | custom-call | tf_op jit(solution)/shard_map/ffn_back/pallas_call | solution.py:583
  141.8 3.2 collective-permute-done.40
  147.8 23.3 %attend_back.1 = (bf16[1024,512]{1,0:T(8,128)(2,1)S(1)}, bf16[1024,512]{1,0:T(8,128)(2,1)S(1)}, bf16[1024,512]{1,0:T(8,128)(2,1)S(1)}) custom-call(s32[1,16]{1,0:T(1,128)S(1)} %copy-done.24, bf16[1024,1536]{1,0:T(8,128)(2,1)} %copy-done, bf16[1024,1536]{1,0:T(8,128)(2,1)} %copy-done, bf16[1024,1536]{1,0:T(8,128)(2,1)} %copy-done, ...), custom_call_target="tpu_custom_call" | custom-call | tf_op jit(solution)/shard_map/attend_back/pallas_call | solution.py:348
  171.1 4.1 %front_back.1 = (bf16[1024,512]{1,0:T(8,128)(2,1)}, f32[2,512]{1,0:T(2,128)S(1)}) custom-call(bf16[1024,512]{1,0:T(8,128)(2,1)S(1)} %get-tuple-element.55.gq.gp_q, bf16[1024,512]{1,0:T(8,128)(2,1)S(1)} %get-tuple-element.56.gk.gp_k, bf16[1024,512]{1,0:T(8,128)(2,1)S(1)} %get-tuple-element.57.gv.gp_v, bf16[512,1536]{1,0:T(8,128)(2,1)S(1)} %copy-done.8, ...), custom_call_target="tpu_custom_call" | custom-call | tf_op jit(solution)/shard_map/front_back/pallas_call | solution.py:647
  196.0 8.1 %down_grad.1 = (bf16[1024,512]{1,0:T(8,128)(2,1)S(1)}, bf16[1024,512]{1,0:T(8,128)(2,1)S(1)}) custom-call(s32[4]{0:T(128)S(1)} %copy-done.21, bf16[1024,2048]{1,0:T(8,128)(2,1)S(1)} %copy-done.9, f32[1024,512]{1,0:T(8,128)S(1)} %copy-done.4), custom_call_target="tpu_custom_call" | custom-call | tf_op jit(solution)/shard_map/down_grad/pallas_call | solution.py:510
  213.3 3.4 collective-permute-start.29
  221.6 3.4 collective-permute-start.32
  227.3 4.5 %collective-permute-done.31 = bf16[2,16,256]{2,1,0:T(8,128)(2,1)S(1)} collective-permute-done((bf16[2,16,256]{2,1,0:T(8,128)(2,1)S(1)}, bf16[2,16,256]{2,1,0:T(8,128)(2,1)S(1)}, u32[]{:S(2)}, u32[]{:S(2)}) %collective-permute-start.31) | collective-permute-done | bytes 16416 | tf_op jit(solution)/shard_map/ppermute | solution.py:712
  245.6 4.8 %collective-permute-done.6 = bf16[128,768]{1,0:T(8,128)(2,1)S(1)} collective-permute-done((bf16[128,768]{1,0:T(8,128)(2,1)S(1)}, bf16[128,768]{1,0:T(8,128)(2,1)S(1)}, u32[]{:S(2)}, u32[]{:S(2)}) %collective-permute-start.6) | collective-permute-done | bytes 196640 | tf_op jit(solution)/shard_map/ppermute | solution.py:712
  257.1 3.3 collective-permute-start.12
  268.4 3.3 collective-permute-done.15
  272.0 4.8 %collective-permute-done.14 = bf16[2,16,768]{2,1,0:T(8,128)(2,1)S(1)} collective-permute-done((bf16[2,16,768]{2,1,0:T(8,128)(2,1)S(1)}, bf16[2,16,768]{2,1,0:T(8,128)(2,1)S(1)}, u32[]{:S(2)}, u32[]{:S(2)}) %collective-permute-start.14) | collective-permute-done | bytes 49184 | tf_op jit(solution)/shard_map/ppermute | solution.py:712
  276.9 4.0 %collective-permute-done.13 = bf16[2,16,768]{2,1,0:T(8,128)(2,1)S(1)} collective-permute-done((bf16[2,16,768]{2,1,0:T(8,128)(2,1)S(1)}, bf16[2,16,768]{2,1,0:T(8,128)(2,1)S(1)}, u32[]{:S(2)}, u32[]{:S(2)}) %collective-permute-start.13) | collective-permute-done | bytes 49184 | tf_op jit(solution)/shard_map/ppermute | solution.py:712
  287.3 3.2 collective-permute-done.18
  324.6 4.0 %collective-permute-done.54 = bf16[2,16,1024]{2,1,0:T(8,128)(2,1)S(1)} collective-permute-done((bf16[2,16,1024]{2,1,0:T(8,128)(2,1)S(1)}, bf16[2,16,1024]{2,1,0:T(8,128)(2,1)S(1)}, u32[]{:S(2)}, u32[]{:S(2)}) %collective-permute-start.54) | collective-permute-done | bytes 65568 | tf_op jit(solution)/shard_map/ppermute | solution.py:712
  333.2 4.3 %collective-permute-done.71 = bf16[2,32,512]{2,1,0:T(8,128)(2,1)S(1)} collective-permute-done((bf16[2,32,512]{2,1,0:T(8,128)(2,1)S(1)}, bf16[2,32,512]{2,1,0:T(8,128)(2,1)S(1)}, u32[]{:S(2)}, u32[]{:S(2)}) %collective-permute-start.71) | collective-permute-done | bytes 65568 | tf_op jit(solution)/shard_map/ppermute | solution.py:712
  354.6 4.1 %collective-permute-done.75 = bf16[256,512]{1,0:T(8,128)(2,1)S(1)} collective-permute-done((bf16[256,512]{1,0:T(8,128)(2,1)S(1)}, bf16[256,512]{1,0:T(8,128)(2,1)S(1)}, u32[]{:S(2)}, u32[]{:S(2)}) %collective-permute-start.75) | collective-permute-done | bytes 262176 | tf_op jit(solution)/shard_map/ppermute | solution.py:712
  367.3 3.3 finish.6
  (334 shorter events, 161.8 us)
Async XLA Ops:
  7.2 63.6 %all-gather.2.cloned.1.call-start = ((), (), s32[]{:S(2)}) async-start(), calls=%async_computation | async-start | bytes 10485760 | tf_op jit(solution)/shard_map/all_gather | solution.py:784
  138.9 66.1 %collective-permute-start.25 = (bf16[128,256]{1,0:T(8,128)(2,1)S(1)}, bf16[128,256]{1,0:T(8,128)(2,1)S(1)}, u32[]{:S(2)}, u32[]{:S(2)}) collective-permute-start(bf16[128,256]{1,0:T(8,128)(2,1)S(1)} %get-tuple-element.85), channel_id=1, source_target_pairs={{0,4},{4,0},{8,12},{12,8},{16,20},{20,16},{24,28},{28,24},{1,5},{5... | collective-permute-start | bytes 196616 | tf_op jit(solution)/shard_map/ppermute | solution.py:712
  145.0 31.8 %collective-permute-start.41 = (f32[8,512]{1,0:T(8,128)S(1)}, f32[8,512]{1,0:T(8,128)S(1)}, u32[]{:S(2)}, u32[]{:S(2)}) collective-permute-start(f32[8,512]{1,0:T(8,128)S(1)} %add.289), channel_id=1, source_target_pairs={{0,4},{4,0},{8,12},{12,8},{16,20},{20,16},{24,28},{28,24},{1,5},{5... | collective-permute-start | bytes 49160 | tf_op jit(solution)/shard_map/ppermute | solution.py:712
  176.8 27.3 %collective-permute-start.42 = (f32[8,512]{1,0:T(8,128)S(1)}, f32[8,512]{1,0:T(8,128)S(1)}, u32[]{:S(2)}, u32[]{:S(2)}) collective-permute-start(f32[8,512]{1,0:T(8,128)S(1)} %add.290), channel_id=1, source_target_pairs={{0,8},{4,12},{8,0},{12,4},{16,24},{20,28},{24,16},{28,20},{1,9},{5... | collective-permute-start | bytes 49160 | tf_op jit(solution)/shard_map/ppermute | solution.py:712
  187.3 16.8 %collective-permute-start.4 = (f32[2,512]{1,0:T(2,128)S(1)}, f32[2,512]{1,0:T(2,128)S(1)}, u32[]{:S(2)}, u32[]{:S(2)}) collective-permute-start(f32[2,512]{1,0:T(2,128)S(1)} %add.256), channel_id=1, source_target_pairs={{0,16},{4,20},{8,24},{12,28},{16,0},{20,4},{24,8},{28,12},{1,17},{... | collective-permute-start | bytes 12296 | tf_op jit(solution)/shard_map/ppermute | solution.py:712
  193.7 44.5 %collective-permute-start.5 = (bf16[256,1536]{1,0:T(8,128)(2,1)S(1)}, bf16[256,1536]{1,0:T(8,128)(2,1)S(1)}, u32[]{:S(2)}, u32[]{:S(2)}) collective-permute-start(bf16[256,1536]{1,0:T(8,128)(2,1)S(1)} %get-tuple-element.63), channel_id=1, source_target_pairs={{0,1},{1,0},{2,3},{3,2},{4,5},{5,4},{6,7},{7,6},{8,9},{9,8},{10,11... | collective-permute-start | bytes 2359304 | tf_op jit(solution)/shard_map/ppermute | solution.py:712
  204.1 14.2 %collective-permute-start.43 = (f32[8,512]{1,0:T(8,128)S(1)}, f32[8,512]{1,0:T(8,128)S(1)}, u32[]{:S(2)}, u32[]{:S(2)}) collective-permute-start(f32[8,512]{1,0:T(8,128)S(1)} %add.291), channel_id=1, source_target_pairs={{0,16},{4,20},{8,24},{12,28},{16,0},{20,4},{24,8},{28,12},{1,17},{... | collective-permute-start | bytes 49160 | tf_op jit(solution)/shard_map/ppermute | solution.py:712
  218.3 34.0 %collective-permute-start.44 = (bf16[256,2048]{1,0:T(8,128)(2,1)S(1)}, bf16[256,2048]{1,0:T(8,128)(2,1)S(1)}, u32[]{:S(2)}, u32[]{:S(2)}) collective-permute-start(bf16[256,2048]{1,0:T(8,128)(2,1)S(1)} %copy-done.34), channel_id=1, source_target_pairs={{0,1},{1,0},{2,3},{3,2},{4,5},{5,4},{6,7},{7,6},{8,9},{9,8},{10,11... | collective-permute-start | bytes 3145736 | tf_op jit(solution)/shard_map/ppermute | solution.py:712
  219.0 41.4 %collective-permute-start.61 = (bf16[1024,512]{1,0:T(8,128)(2,1)S(1)}, bf16[1024,512]{1,0:T(8,128)(2,1)S(1)}, u32[]{:S(2)}, u32[]{:S(2)}) collective-permute-start(bf16[1024,512]{1,0:T(8,128)(2,1)S(1)} %get-tuple-element.71), channel_id=1, source_target_pairs={{0,1},{1,0},{2,3},{3,2},{4,5},{5,4},{6,7},{7,6},{8,9},{9,8},{10,11... | collective-permute-start | bytes 3145736 | tf_op jit(solution)/shard_map/ppermute | solution.py:712
  221.4 10.4 %collective-permute-start.30 = (bf16[2,16,256]{2,1,0:T(8,128)(2,1)S(1)}, bf16[2,16,256]{2,1,0:T(8,128)(2,1)S(1)}, u32[]{:S(2)}, u32[]{:S(2)}) collective-permute-start(bf16[2,16,256]{2,1,0:T(8,128)(2,1)S(1)} %add_convert_fusion.43), channel_id=1, source_target_pairs={{0,8},{4,12},{8,0},{12,4},{16,24},{20,28},{24,16},{28,20},{1,9},{5... | collective-permute-start | bytes 49160 | tf_op jit(solution)/shard_map/ppermute | solution.py:712
  240.4 118.4 %collective-permute-start.37 = (bf16[256,256]{1,0:T(8,128)(2,1)S(1)}, bf16[256,256]{1,0:T(8,128)(2,1)S(1)}, u32[]{:S(2)}, u32[]{:S(2)}) collective-permute-start(bf16[256,256]{1,0:T(8,128)(2,1)S(1)} %constant_dynamic-update-slice_fusion.27.own_a), channel_id=1, source_target_pairs={{0,1},{1,0},{2,3},{3,2},{4,5},{5,4},{6,7},{7,6},{8,9},{9,8},{10,11... | collective-permute-start | bytes 393224 | tf_op jit(solution)/shard_map/ppermute | solution.py:712
  241.5 117.8 %collective-permute-start.38 = (bf16[256,256]{1,0:T(8,128)(2,1)S(1)}, bf16[256,256]{1,0:T(8,128)(2,1)S(1)}, u32[]{:S(2)}, u32[]{:S(2)}) collective-permute-start(bf16[256,256]{1,0:T(8,128)(2,1)S(1)} %constant_dynamic-update-slice_fusion.38.own_b), channel_id=1, source_target_pairs={{0,1},{1,0},{2,3},{3,2},{4,5},{5,4},{6,7},{7,6},{8,9},{9,8},{10,11... | collective-permute-start | bytes 393224 | tf_op jit(solution)/shard_map/ppermute | solution.py:712
  263.0 29.0 %collective-permute-start.47 = (bf16[128,1024]{1,0:T(8,128)(2,1)S(1)}, bf16[128,1024]{1,0:T(8,128)(2,1)S(1)}, u32[]{:S(2)}, u32[]{:S(2)}) collective-permute-start(bf16[128,1024]{1,0:T(8,128)(2,1)S(1)} %get-tuple-element.77), channel_id=1, source_target_pairs={{0,4},{4,0},{8,12},{12,8},{16,20},{20,16},{24,28},{28,24},{1,5},{5... | collective-permute-start | bytes 786440 | tf_op jit(solution)/shard_map/ppermute | solution.py:712
  265.4 27.2 %collective-permute-start.45 = (bf16[128,1024]{1,0:T(8,128)(2,1)S(1)}, bf16[128,1024]{1,0:T(8,128)(2,1)S(1)}, u32[]{:S(2)}, u32[]{:S(2)}) collective-permute-start(bf16[128,1024]{1,0:T(8,128)(2,1)S(1)} %get-tuple-element.79), channel_id=1, source_target_pairs={{0,2},{1,3},{2,0},{3,1},{4,6},{5,7},{6,4},{7,5},{8,10},{9,11},{10,... | collective-permute-start | bytes 786440 | tf_op jit(solution)/shard_map/ppermute | solution.py:712
  292.6 16.7 %collective-permute-start.17 = (bf16[128,768]{1,0:T(8,128)(2,1)S(1)}, bf16[128,768]{1,0:T(8,128)(2,1)S(1)}, u32[]{:S(2)}, u32[]{:S(2)}) collective-permute-start(bf16[128,768]{1,0:T(8,128)(2,1)S(1)} %get-tuple-element.114), channel_id=1, source_target_pairs={{0,2},{1,3},{2,0},{3,1},{4,6},{5,7},{6,4},{7,5},{8,10},{9,11},{10,... | collective-permute-start | bytes 589832 | tf_op jit(solution)/shard_map/ppermute | solution.py:712
  319.9 11.5 %collective-permute-start.52 = (bf16[2,16,1024]{2,1,0:T(8,128)(2,1)S(1)}, bf16[2,16,1024]{2,1,0:T(8,128)(2,1)S(1)}, u32[]{:S(2)}, u32[]{:S(2)}) collective-permute-start(bf16[2,16,1024]{2,1,0:T(8,128)(2,1)S(1)} %add_convert_fusion.31), channel_id=1, source_target_pairs={{0,8},{4,12},{8,0},{12,4},{16,24},{20,28},{24,16},{28,20},{1,9},{5... | collective-permute-start | bytes 196616 | tf_op jit(solution)/shard_map/ppermute | solution.py:712
  328.6 11.1 %collective-permute-start.69 = (bf16[2,32,512]{2,1,0:T(8,128)(2,1)S(1)}, bf16[2,32,512]{2,1,0:T(8,128)(2,1)S(1)}, u32[]{:S(2)}, u32[]{:S(2)}) collective-permute-start(bf16[2,32,512]{2,1,0:T(8,128)(2,1)S(1)} %add_convert_fusion.30), channel_id=1, source_target_pairs={{0,8},{4,12},{8,0},{12,4},{16,24},{20,28},{24,16},{28,20},{1,9},{5... | collective-permute-start | bytes 196616 | tf_op jit(solution)/shard_map/ppermute | solution.py:712
  329.6 8.7 %collective-permute-start.70 = (bf16[2,32,512]{2,1,0:T(8,128)(2,1)S(1)}, bf16[2,32,512]{2,1,0:T(8,128)(2,1)S(1)}, u32[]{:S(2)}, u32[]{:S(2)}) collective-permute-start(bf16[2,32,512]{2,1,0:T(8,128)(2,1)S(1)} %add_convert_fusion.30), channel_id=1, source_target_pairs={{0,16},{4,20},{8,24},{12,28},{16,0},{20,4},{24,8},{28,12},{1,17},{... | collective-permute-start | bytes 196616 | tf_op jit(solution)/shard_map/ppermute | solution.py:712
  350.2 8.5 %collective-permute-start.75 = (bf16[256,512]{1,0:T(8,128)(2,1)S(1)}, bf16[256,512]{1,0:T(8,128)(2,1)S(1)}, u32[]{:S(2)}, u32[]{:S(2)}) collective-permute-start(bf16[256,512]{1,0:T(8,128)(2,1)S(1)} %get-tuple-element.88), channel_id=1, source_target_pairs={{0,4},{4,0},{8,12},{12,8},{16,20},{20,16},{24,28},{28,24},{1,5},{5... | collective-permute-start | bytes 786440 | tf_op jit(solution)/shard_map/ppermute | solution.py:712
  351.2 9.7 %collective-permute-start.20 = (bf16[256,768]{1,0:T(8,128)(2,1)S(1)}, bf16[256,768]{1,0:T(8,128)(2,1)S(1)}, u32[]{:S(2)}, u32[]{:S(2)}) collective-permute-start(bf16[256,768]{1,0:T(8,128)(2,1)S(1)} %constant_dynamic-update-slice_fusion.5.own_a), channel_id=1, source_target_pairs={{0,1},{1,0},{2,3},{3,2},{4,5},{5,4},{6,7},{7,6},{8,9},{9,8},{10,11... | collective-permute-start | bytes 1179656 | tf_op jit(solution)/shard_map/ppermute | solution.py:712
  358.7 8.5 %collective-permute-start.59 = (bf16[256,1024]{1,0:T(8,128)(2,1)S(1)}, bf16[256,1024]{1,0:T(8,128)(2,1)S(1)}, u32[]{:S(2)}, u32[]{:S(2)}) collective-permute-start(bf16[256,1024]{1,0:T(8,128)(2,1)S(1)} %constant_dynamic-update-slice_fusion.49.own_a), channel_id=1, source_target_pairs={{0,1},{1,0},{2,3},{3,2},{4,5},{5,4},{6,7},{7,6},{8,9},{9,8},{10,11... | collective-permute-start | bytes 1572872 | tf_op jit(solution)/shard_map/ppermute | solution.py:712
  358.8 8.5 %collective-permute-start.60 = (bf16[256,1024]{1,0:T(8,128)(2,1)S(1)}, bf16[256,1024]{1,0:T(8,128)(2,1)S(1)}, u32[]{:S(2)}, u32[]{:S(2)}) collective-permute-start(bf16[256,1024]{1,0:T(8,128)(2,1)S(1)} %constant_dynamic-update-slice_fusion.60.own_b), channel_id=1, source_target_pairs={{0,1},{1,0},{2,3},{3,2},{4,5},{5,4},{6,7},{7,6},{8,9},{9,8},{10,11... | collective-permute-start | bytes 1572872 | tf_op jit(solution)/shard_map/ppermute | solution.py:712
  359.3 11.2 %collective-permute-start.76 = (bf16[512,512]{1,0:T(8,128)(2,1)S(1)}, bf16[512,512]{1,0:T(8,128)(2,1)S(1)}, u32[]{:S(2)}, u32[]{:S(2)}) collective-permute-start(bf16[512,512]{1,0:T(8,128)(2,1)S(1)} %constant_dynamic-update-slice_fusion.71.own_a), channel_id=1, source_target_pairs={{0,1},{1,0},{2,3},{3,2},{4,5},{5,4},{6,7},{7,6},{8,9},{9,8},{10,11... | collective-permute-start | bytes 1572872 | tf_op jit(solution)/shard_map/ppermute | solution.py:712
  360.8 9.7 %collective-permute-start.77 = (bf16[512,512]{1,0:T(8,128)(2,1)S(1)}, bf16[512,512]{1,0:T(8,128)(2,1)S(1)}, u32[]{:S(2)}, u32[]{:S(2)}) collective-permute-start(bf16[512,512]{1,0:T(8,128)(2,1)S(1)} %constant_dynamic-update-slice_fusion.82.own_b), channel_id=1, source_target_pairs={{0,1},{1,0},{2,3},{3,2},{4,5},{5,4},{6,7},{7,6},{8,9},{9,8},{10,11... | collective-permute-start | bytes 1572872 | tf_op jit(solution)/shard_map/ppermute | solution.py:712
  (90 other events, 608.8 us)
Sparse Core Ops, SparseCore 0:
  9.6 61.1 all-gather.1
